TPU v7x, 128 devices: a whole 4x4x4 slice. The times are simulated.
128 devices in a mesh: seq: 32 (over y, z_hi, x), tp: 4 (over z_lo, core).
Axes of the slice: x: 4, y: 4, z: 4 (z_hi: 2, z_lo: 2; z = z_hi * 2 + z_lo), core: 2. Of those that a mesh axis runs over, the one named last changes fastest.
Arguments:
- query: bfloat16 [4096, 36864], P('seq', 'tp'), may hold values from -40 to 40
- latent: bfloat16 [4096, 576], P(('seq', 'tp')), may hold values from -5 to 5
- out_grad: bfloat16 [4096, 32768], P('seq', 'tp'), may hold values from -6 to 6
- positions: int32 [4096], P('seq'), may hold values from 0 to 4095, as said below
Outputs:
- query_grad: bfloat16 [4096, 36864], P('seq', 'tp')
- latent_grad: float32 [4096, 576], P(('seq', 'tp'))
Inputs may be any that keep to these rules, and one draw needn't show every extreme that they name: positions is a permutation of 0 to 4095 made of aligned runs of 64 rows, each run holding 64 consecutive values in increasing order.
All inputs are finite; a program needn't handle non-finite values.
Results may differ from a plain program's by a relative error of at most 0.0047.
Values may be sent and summed in bfloat16 or wider, within the bound.
A program may use at most 192 MiB of HBM per device.

v0:
```python
import jax
import jax.numpy as jnp
from jax import lax
from jax.sharding import PartitionSpec as P

LAT = 512
KVW = 576


softmax_scale = 192.0 ** (-0.5)
masked_score = -1e30


def per_device(query, latent, out_grad, positions):
    share = latent.shape[0]
    tok_rows = query.shape[0]
    heads_dev = query.shape[1] // KVW
    own_places = lax.dynamic_slice_in_dim(positions, lax.axis_index("tp") * share, share)
    key_rows, key_places = (
        lax.all_gather(latent, ("seq", "tp"), axis=0, tiled=True),
        lax.all_gather(own_places, ("seq", "tp"), axis=0, tiled=True),
    )
    query_heads = query.reshape(tok_rows, heads_dev, KVW)
    grad_heads = out_grad.reshape(tok_rows, heads_dev, LAT)
    values = key_rows[:, :LAT]
    scores = (
        jnp.einsum("ihd,jd->hij", query_heads, key_rows, preferred_element_type=jnp.float32)
        * softmax_scale
    )
    visible = key_places[None, :] <= positions[:, None]
    scores = jnp.where(visible[None], scores, masked_score)
    row_top = jnp.max(scores, axis=2, keepdims=True)
    exponent = jnp.exp(scores - row_top)
    weights = exponent / jnp.sum(exponent, axis=2, keepdims=True)
    weights_half = weights.astype(jnp.bfloat16)
    grad_weights = jnp.einsum("ihl,jl->hij", grad_heads, values, preferred_element_type=jnp.float32)
    row_delta = jnp.sum(weights * grad_weights, axis=2, keepdims=True)
    grad_scores = (weights * (grad_weights - row_delta) * softmax_scale).astype(jnp.bfloat16)
    head_qgrad = jnp.einsum(
        "hij,jd->ihd", grad_scores, key_rows, preferred_element_type=jnp.float32
    )
    query_grad = head_qgrad.astype(jnp.bfloat16).reshape(tok_rows, heads_dev * KVW)
    key_grad = jnp.einsum(
        "hij,ihd->jd", grad_scores, query_heads, preferred_element_type=jnp.float32
    )
    value_grad = jnp.einsum(
        "hij,ihl->jl", weights_half, grad_heads, preferred_element_type=jnp.float32
    )
    terms = key_grad + jnp.pad(value_grad, ((0, 0), (0, KVW - LAT)))
    reduced = lax.psum_scatter(terms, "seq", scatter_dimension=0, tiled=True)
    latent_grad = lax.psum_scatter(reduced, "tp", scatter_dimension=0, tiled=True)
    return (query_grad, latent_grad)


def solution(mesh):
    return jax.shard_map(
        per_device,
        mesh=mesh,
        in_specs=(P("seq", "tp"), P(("seq", "tp"), None), P("seq", "tp"), P("seq")),
        out_specs=(P("seq", "tp"), P(("seq", "tp"), None)),
        check_vma=False,
    )
```

profile of v0, /device:TPU:0, one launch (start us, length us, event | category | flops | bytes accessed | tf_op | source)
XLA Modules:
  0.0 671.1 jit_solution(169204800546690262)
XLA Ops:
  7.2 0.0 all-gather.2.cloned.1.call-start
  7.2 0.7 all-gather.2.cloned.1.call-update
  7.9 0.0 reduce-scatter.5.cloned.1.call-start
  7.9 3.0 copy.23
  11.0 4.1 copy.36
  15.1 0.8 dynamic-slice_dynamic-update-slice_fusion
  15.9 68.2 %all-reduce.1 = s32[4096]{0:T(1024)S(1)} all-reduce(s32[4096]{0:T(1024)S(1)} %dynamic-slice_dynamic-update-slice_fusion), channel_id=1, replica_groups=mesh['seq'=32,'tp'=4] {'seq','tp'}, use_global_device_ids=true, to_apply=%add.1 | all-reduce | flops 4096 | bytes 32768
  84.1 2.5 broadcast_compare_fusion
  86.6 126.0 %all-gather.2.cloned.1.call-done = bf16[4096,576]{1,0:T(8,128)(2,1)} async-done(((bf16[32,576]{1,0:T(8,128)(2,1)}), bf16[4096,576]{1,0:T(8,128)(2,1)}) %all-gather.2.cloned.1.call-update) | async-done | bytes 4718608 | tf_op jit(solution)/shard_map/all_gather | solution.py:20
  212.6 19.5 %fusion.18 = f32[4096,128,16]{1,0,2:T(8,128)} fusion(bf16[128,16,576]{0,2,1:T(8,128)(2,1)S(1)} %bitcast.71, bf16[4096,576]{1,0:T(8,128)(2,1)} %all-gather.2.cloned.1.call-done), kind=kOutput, calls=%fused_computation.22 | convolution fusion | flops 9663676416 | bytes 40632320 | tf_op jit(solution)/shard_map/ihd,jd->hij/dot_general | solution.py:27
  232.1 38.1 %fusion.30 = (f32[16,128]{1,0:T(8,128)S(1)}, f32[16,128,4096]{1,2,0:T(8,128)}) fusion(f32[4096,128,16]{1,0,2:T(8,128)} %fusion.18, pred[128,4096]{0,1:T(8,128)(4,1)S(1)} %broadcast_compare_fusion), kind=kOutput, calls=%fused_computation.35 | output fusion | flops 50335744 | bytes 67641344 | tf_op jit(solution)/shard_map/sub | solution.py:33
  270.2 17.7 %fusion.14 = f32[4096,512]{0,1:T(8,128)} fusion(bf16[128,16,512]{0,2,1:T(8,128)(2,1)} %bitcast.74, f32[16,128,4096]{1,2,0:T(8,128)} %get-tuple-element.9, f32[16,128]{1,0:T(8,128)S(1)} %get-tuple-element.8), kind=kOutput, calls=%fused_computation.20 | convolution fusion | flops 8606711808 | bytes 44048384 | tf_op jit(solution)/shard_map/hij,ihl->jl/dot_general | solution.py:46
  287.8 17.7 %fusion.20 = f32[4096,128,16]{1,0,2:T(8,128)} fusion(bf16[128,16,512]{0,2,1:T(8,128)(2,1)} %bitcast.75, bf16[4096,576]{1,0:T(8,128)(2,1)} %all-gather.2.cloned.1.call-done), kind=kOutput, calls=%fused_computation.25 | convolution fusion | flops 8589934592 | bytes 39845888 | tf_op jit(solution)/shard_map/ihl,jl->hij/dot_general | solution.py:36
  305.6 59.6 %bitcast_add_fusion = f32[4096,576]{0,1:T(8,128)} fusion(f32[4096,512]{0,1:T(8,128)} %fusion.14, bf16[128,16,576]{0,2,1:T(8,128)(2,1)S(1)} %bitcast.72, f32[4096,128,16]{1,0,2:T(8,128)} %fusion.20, f32[16,128,4096]{1,2,0:T(8,128)} %get-tuple-element.9, f32[16,128]{1,0:T(8,128)S(1)} %get-tuple-element.8), kind=kOutput, calls=%fused_computation.17 | convolution fusion | flops 9724762112 | bytes 87302144 | tf_op jit(solution)/shard_map/hij,ihd->jd/dot_general | solution.py:43
  365.2 0.0 reduce-scatter.5.cloned.1.call-update
  365.2 0.0 reduce-scatter.7.cloned.1.call-start
  365.2 240.3 %reduce-scatter.5.cloned.1.call-done = f32[128,576]{0,1:T(8,128)} async-done(((f32[4096,576]{0,1:T(8,128)}), f32[128,576]{0,1:T(8,128)}) %reduce-scatter.5.cloned.1.call-update) | async-done | bytes 294928 | tf_op jit(solution)/shard_map/reduce_scatter | solution.py:50
  605.6 1.8 copy.34
  607.4 0.0 reduce-scatter.7.cloned.1.call-update
  607.5 54.6 %fusion.21 = bf16[16,128,576]{1,2,0:T(8,128)(2,1)S(1)} fusion(bf16[4096,576]{1,0:T(8,128)(2,1)} %all-gather.2.cloned.1.call-done, f32[4096,128,16]{1,0,2:T(8,128)} %fusion.20, f32[16,128,4096]{1,2,0:T(8,128)} %get-tuple-element.9, f32[16,128]{1,0:T(8,128)S(1)} %get-tuple-element.8), kind=kOutput, calls=%fused_computation.26 | convolution fusion | flops 9723582464 | bytes 74194944 | tf_op jit(solution)/shard_map/hij,jd->ihd/dot_general | solution.py:39
  662.1 2.4 copy.29
  664.5 0.0 reduce-scatter.7.cloned.1.call-done
  (1 shorter events, 0.0 us)
Async XLA Ops:
  7.2 205.5 %all-gather.2.cloned.1.call-start = ((), (), s32[]{:S(2)}) async-start(), calls=%async_computation.2 | async-start | bytes 5283840 | tf_op jit(solution)/shard_map/all_gather | solution.py:20
  7.9 597.7 %reduce-scatter.5.cloned.1.call-start = ((), (), s32[]{:S(2)}) async-start(), calls=%async_computation.3 | async-start | bytes 9732096 | tf_op jit(solution)/shard_map/reduce_scatter | solution.py:50
  365.2 299.3 %reduce-scatter.7.cloned.1.call-start = ((), (), s32[]{:S(2)}) async-start(), calls=%async_computation.4 | async-start | bytes 409600
Sparse Core Ops, SparseCore 0:
  9.7 202.8 all-gather.1
  365.3 240.2 reduce-scatter.4
  608.7 14.4 reduce-scatter.6
where the time goes:
time: 671 us
  waiting for transfers between devices  367 us (55%)
  matrix products  169 us (25%)
  blocking collectives  68.2 us (10%)
  other arithmetic  40.6 us (6%)
  between operations  13.8 us (2%)
  local copies, waits for them, and re-layouts  12.2 us (2%)
    reduce_scatter x1, waiting for transfers between devices, per_device(): reduced = lax.psum_scatter(terms, 'seq', scatter_dimension=0, tiled=True)  240 us
    all_gather x1, waiting for transfers between devices, per_device(): lax.all_gather(latent, ('seq', 'tp'), axis=0, tiled=True)  126 us
    unnamed x1, blocking collectives  68.2 us
    dot_general x1, matrix products, per_device(): jnp.einsum('hij,ihd->jd', grad_scores, query_heads, preferred_element_typ...  59.6 us
    dot_general x1, matrix products, per_device(): jnp.einsum('hij,jd->ihd', grad_scores, key_rows, preferred_element_type=j...  54.6 us
    sub x1, other arithmetic, per_device(): exponent = jnp.exp(scores - row_top)  38.1 us
    dot_general x1, matrix products, per_device(): jnp.einsum('ihd,jd->hij', query_heads, key_rows, preferred_element_type=j...  19.5 us
    dot_general x1, matrix products, per_device(): jnp.einsum('ihl,jl->hij', grad_heads, values, preferred_element_type=jnp....  17.7 us
  transfers between devices with their start and end apart: 3, of which 2 were waited for; matrix products, arithmetic and copies ran while one was open for 10% of the time, Pallas kernels for 0%

commit v1 on v0

v1 whole, which is shorter than its diff:
```python
import functools
import math

import jax, jax.numpy as jnp
from jax import lax
from jax.experimental import pallas as pl
from jax.experimental.pallas import tpu as pltpu
from jax.sharding import PartitionSpec as P

LAT=512; KVW=576; PAD=640
MESH = pl.DeviceIdType.MESH
PARTS = (((0, 1, 2), 0, 256), ((1, 2, 0), 256, 256), ((2, 0, 1), 512, 128))


def coords():
    seq, tp = lax.axis_index("seq"), lax.axis_index("tp")
    x = lax.rem(seq, 4)
    z = lax.rem(seq // 4, 2) * 2 + tp // 2
    y = seq // 8
    return [x, y, z], lax.rem(tp, 2)


def device(place, core):
    x, y, z = place
    return ((y * 2 + z // 2) * 4 + x, lax.rem(z, 2) * 2 + core)


def moved(place, axis, by):
    out = list(place)
    out[axis] = lax.rem(place[axis] + by, 4)
    return out


def greet(place, core):
    barrier = pltpu.get_barrier_semaphore()
    for axis in range(3):
        for by in (1, 3):
            pl.semaphore_signal(barrier, inc=1, device_id=device(moved(place, axis, by), core), device_id_type=MESH)
    pl.semaphore_signal(barrier, inc=1, device_id=device(place, 1 - core), device_id_type=MESH)
    pl.semaphore_wait(barrier, 7)


def gather_kernel(pos_ref, lat_ref, out_ref, own, sem, send, recv):
    place, core = coords()
    greet(place, core)
    run = pos_ref[lax.rem(place[2], 2) * 64] // 64
    own[:, :KVW] = lat_ref[...]
    own[:, KVW:] = jnp.full((32, PAD - KVW), run.astype(jnp.float32)).astype(jnp.bfloat16)
    put = pltpu.make_async_copy(own, out_ref.at[core, place[0], place[1], place[2]], sem)
    put.start()
    put.wait()
    count = [0]
    sent = []

    def copy(ref, dev):
        i = count[0]
        count[0] += 1
        c = pltpu.make_async_remote_copy(ref, ref, send.at[i], recv.at[i], device_id=dev, device_id_type=MESH)
        c.start()
        sent.append(c)
        return c

    def view(done, axis, value, rows, lane, width):
        at = [pl.ds(0, 4) if a in done else place[a] for a in range(3)]
        at[axis] = value
        return out_ref.at[core, at[0], at[1], at[2], pl.ds(*rows), pl.ds(lane, width)]

    both = (0, 32)
    sibling = device(place, 1 - core)
    twins = []
    twins.append(copy(out_ref.at[core, place[0], place[1], place[2]], sibling))
    for phase in range(3):
        first = []
        for order, lane, width in PARTS:
            axis, done = order[phase], order[:phase]
            mine = view(done, axis, place[axis], both, lane, width)
            r = copy(mine, device(moved(place, axis, 1), core))
            l = copy(mine, device(moved(place, axis, 3), core))
            first.append((r, l))
        second = []
        for (order, lane, width), (r, l) in zip(PARTS, first):
            axis, done = order[phase], order[:phase]
            right, left = lax.rem(place[axis] + 1, 4), lax.rem(place[axis] + 3, 4)
            r.wait_recv()
            a = copy(view(done, axis, left, (0, 16), lane, width), device(moved(place, axis, 1), core))
            l.wait_recv()
            b = copy(view(done, axis, right, (16, 16), lane, width), device(moved(place, axis, 3), core))
            twins.append(copy(view(done, axis, left, both, lane, width), sibling))
            twins.append(copy(view(done, axis, right, both, lane, width), sibling))
            second.append((a, b))
        for (order, lane, width), (a, b) in zip(PARTS, second):
            axis, done = order[phase], order[:phase]
            a.wait_recv()
            b.wait_recv()
            twins.append(copy(view(done, axis, lax.rem(place[axis] + 2, 4), both, lane, width), sibling))
    for t in twins:
        t.wait_recv()
    for s in sent:
        s.wait_send()


N_GATHER = 1 + 3 * 3 * 7


def gather(positions, latent):
    return pl.pallas_call(
        gather_kernel,
        out_shape=jax.ShapeDtypeStruct((2, 4, 4, 4, 32, PAD), jnp.bfloat16),
        in_specs=[pl.BlockSpec(memory_space=pltpu.SMEM), pl.BlockSpec(memory_space=pltpu.VMEM)],
        out_specs=pl.BlockSpec(memory_space=pl.ANY),
        scratch_shapes=[
            pltpu.VMEM((32, PAD), jnp.bfloat16),
            pltpu.SemaphoreType.DMA,
            pltpu.SemaphoreType.DMA((N_GATHER,)),
            pltpu.SemaphoreType.DMA((N_GATHER,)),
        ],
        compiler_params=pltpu.CompilerParams(collective_id=0, has_side_effects=True),
        cost_estimate=pl.CostEstimate(flops=0, bytes_accessed=10 * 2**20, transcendentals=0),
        name="gather_latent",
    )(positions, latent)


def dropped(axis, done):
    return axis - sum(1 for a in done if a < axis)


def at(ref, dim, value, rows=None):
    index = [slice(None)] * dim + [value]
    view = ref.at[tuple(index)]
    if rows is not None:
        lead = len(view.shape) - 2
        view = view.at[tuple([slice(None)] * lead + [pl.ds(*rows)])]
    return view


def scatter_kernel(wires, part_ref, out_ref, mine, theirs, keep, wire, relay, landed, sem, send, recv):
    place, core = coords()
    greet(place, core)
    count = [0]
    sent = []

    def copy(src, dst, dev):
        i = count[0]
        count[0] += 1
        c = pltpu.make_async_remote_copy(src, dst, send.at[i], recv.at[i], device_id=dev, device_id_type=MESH)
        c.start()
        sent.append(c)
        return c

    sibling = device(place, 1 - core)
    swaps, loads = [], []
    for n, (order, lane, width) in enumerate(PARTS):
        other = part_ref.at[:, :, :, pl.ds(32 * (1 - core), 32), pl.ds(lane, width)]
        swaps.append(copy(other, theirs[n], sibling))
        load = pltpu.make_async_copy(part_ref.at[:, :, :, pl.ds(32 * core, 32), pl.ds(lane, width)], mine[n], sem.at[n])
        load.start()
        loads.append(load)

    halves = ((0, 16), (16, 16))
    for phase in range(3):
        started = []
        for n, (order, lane, width) in enumerate(PARTS):
            axis, done = order[phase], order[:phase]
            dim = dropped(axis, done)
            k, w, rl, ld = keep[n][phase], wire[n][phase], relay[n][phase], landed[n][phase]
            me = place[axis]
            right, left, opp = (lax.rem(me + i, 4) for i in (1, 3, 2))
            rdev, ldev = device(moved(place, axis, 1), core), device(moved(place, axis, 3), core)
            if phase == 0:
                loads[n].wait()
                swaps[n].wait_recv()
                def fill(v):
                    at(k, dim, v)[...] = at(mine[n], dim, v)[...].astype(jnp.float32) + at(theirs[n], dim, v)[...].astype(jnp.float32)
            else:
                def fill(v):
                    pass
            fill(opp)
            at(w, dim, opp)[...] = at(k, dim, opp)[...].astype(w.dtype)
            c0 = copy(at(w, dim, opp, halves[0]), rl.at[0], rdev)
            c1 = copy(at(w, dim, opp, halves[1]), rl.at[1], ldev)
            fill(right)
            at(w, dim, right, halves[1])[...] = at(k, dim, right, halves[1])[...].astype(w.dtype)
            c2 = copy(at(w, dim, right, halves[1]), ld.at[0, 1], rdev)
            fill(left)
            at(w, dim, left, halves[0])[...] = at(k, dim, left, halves[0])[...].astype(w.dtype)
            c3 = copy(at(w, dim, left, halves[0]), ld.at[1, 0], ldev)
            fill(me)
            started.append((c0, c1, c2, c3))
        ended = []
        for n, (order, lane, width) in enumerate(PARTS):
            axis, done = order[phase], order[:phase]
            dim = dropped(axis, done)
            k, w, rl, ld = keep[n][phase], wire[n][phase], relay[n][phase], landed[n][phase]
            me = place[axis]
            right, left = lax.rem(me + 1, 4), lax.rem(me + 3, 4)
            rdev, ldev = device(moved(place, axis, 1), core), device(moved(place, axis, 3), core)
            c0, c1, c2, c3 = started[n]
            c0.wait_recv()
            at(w, dim, right, halves[0])[...] = (at(k, dim, right, halves[0])[...] + rl[0].astype(jnp.float32)).astype(w.dtype)
            c4 = copy(at(w, dim, right, halves[0]), ld.at[0, 0], rdev)
            c1.wait_recv()
            at(w, dim, left, halves[1])[...] = (at(k, dim, left, halves[1])[...] + rl[1].astype(jnp.float32)).astype(w.dtype)
            c5 = copy(at(w, dim, left, halves[1]), ld.at[1, 1], ldev)
            ended.append((c2, c3, c4, c5))
        for n, (order, lane, width) in enumerate(PARTS):
            axis, done = order[phase], order[:phase]
            dim = dropped(axis, done)
            k, ld = keep[n][phase], landed[n][phase]
            for c in ended[n]:
                c.wait_recv()
            for h in (0, 1):
                total = (at(k, dim, place[axis], halves[h])[...] + ld[0, h].astype(jnp.float32)) + ld[1, h].astype(jnp.float32)
                if phase < 2:
                    to = keep[n][phase + 1]
                    to.at[tuple([slice(None)] * (2 - phase) + [pl.ds(*halves[h])])][...] = total
                else:
                    real = min(width, KVW - lane)
                    out_ref[pl.ds(*halves[h]), pl.ds(lane, real)] = total[:, :real]
    for s in sent:
        s.wait_send()


N_SCATTER = 3 + 9 * 6


def scatter(part, wires=(jnp.bfloat16, jnp.float32, jnp.float32)):
    V = pltpu.VMEM
    mine = [V((4, 4, 4, 32, w), jnp.bfloat16) for _, _, w in PARTS]
    keep = [[V((4,) * (3 - p) + (32, w), jnp.float32) for p in range(3)] for _, _, w in PARTS]
    wire = [[V((4,) * (3 - p) + (32, w), wires[p]) for p in range(3)] for _, _, w in PARTS]
    relay = [[V((2,) + (4,) * (2 - p) + (16, w), wires[p]) for p in range(3)] for _, _, w in PARTS]
    landed = [[V((2, 2) + (4,) * (2 - p) + (16, w), wires[p]) for p in range(3)] for _, _, w in PARTS]
    return pl.pallas_call(
        functools.partial(scatter_kernel, wires),
        out_shape=jax.ShapeDtypeStruct((32, KVW), jnp.float32),
        in_specs=[pl.BlockSpec(memory_space=pl.ANY)],
        out_specs=pl.BlockSpec(memory_space=pltpu.VMEM),
        scratch_shapes=[
            mine, list(mine), keep, wire, relay, landed,
            pltpu.SemaphoreType.DMA((3,)),
            pltpu.SemaphoreType.DMA((N_SCATTER,)),
            pltpu.SemaphoreType.DMA((N_SCATTER,)),
        ],
        compiler_params=pltpu.CompilerParams(collective_id=1, has_side_effects=True, vmem_limit_bytes=40 * 2**20),
        cost_estimate=pl.CostEstimate(flops=0, bytes_accessed=10 * 2**20, transcendentals=0),
        name="scatter_latent_grad",
    )(part)


SCALE = 192.0 ** -0.5
TO_BASE_2 = SCALE * math.log2(math.e)
MASKED = -1e30
TOKENS = 4096
RUN = 64
RUNS = TOKENS // RUN
HEADS = 16
GROUP = 8
ROWS = GROUP * RUN
BIG, SMALL = 1024, 512


def attend_kernel(chip_run, own_run, q_ref, do_ref, kg_ref, qg_ref, part_ref,
                  chip_of, keys, keys_t, acc, exps, gws, tops, qs, qs_t, dos, dos_t, qg_t, q_in, do_in, qg_out,
                  key_sem, in_sem, out_sem):
    f32, bf16 = jnp.float32, jnp.bfloat16
    copy_q = pltpu.make_async_copy(q_ref, q_in, in_sem.at[0])
    copy_do = pltpu.make_async_copy(do_ref, do_in, in_sem.at[1])

    def place(chip, _):
        run = chip_run[chip]
        chip_of[run] = chip
        for c in range(2):
            pltpu.make_async_copy(kg_ref.at[c, chip], keys.at[pl.ds(run * RUN + c * 32, 32)], key_sem).start()
        return 0

    lax.fori_loop(0, RUNS, place, 0)
    copy_q.start()
    copy_do.start()
    acc[...] = jnp.zeros_like(acc)
    qs[:, LAT:] = jnp.zeros((ROWS, PAD - LAT), bf16)
    pltpu.make_async_copy(keys, keys, key_sem).wait()

    def turn(j, _):
        o = pl.multiple_of(j * 256, 256)
        keys_t[:, pl.ds(o, 256)] = keys[pl.ds(o, 256), :].T
        return 0

    lax.fori_loop(0, TOKENS // 256, turn, 0)
    copy_q.wait()
    copy_do.wait()

    def chunk(c, _):
        half, block = lax.rem(c, 2), c // 2
        run = own_run[block]
        row = pl.multiple_of(block * RUN, RUN)
        for h in range(0, GROUP, 2):
            v = q_in[pl.ds(row, RUN), pl.ds(pl.multiple_of(half * (GROUP * KVW) + h * KVW, 128), 2 * KVW)]
            qs[h * RUN:h * RUN + RUN, :KVW] = v[:, :KVW]
            qs[h * RUN + RUN:h * RUN + 2 * RUN, :KVW] = v[:, KVW:]
            d = do_in[pl.ds(row, RUN), pl.ds(pl.multiple_of(half * (GROUP * LAT) + h * LAT, 128), 2 * LAT)]
            dos[h * RUN:h * RUN + RUN, :] = d[:, :LAT]
            dos[h * RUN + RUN:h * RUN + 2 * RUN, :] = d[:, LAT:]
        qs_t[...] = qs[...].T
        dos_t[...] = dos[...].T
        small = run // (SMALL // RUN)
        bulk = small // 2

        def scan(t, size, masked, carry):
            m, l, d = carry
            o = pl.multiple_of(t * BIG, BIG)
            tile = keys[pl.ds(o, size), :]
            s = jnp.dot(tile, qs_t[...], preferred_element_type=f32)
            g = jnp.dot(tile[:, :LAT], dos_t[...], preferred_element_type=f32)
            if masked:
                key = lax.broadcasted_iota(jnp.int32, (size, ROWS), 0)
                tok = lax.broadcasted_iota(jnp.int32, (size, ROWS), 1) % RUN
                s = jnp.where(key - tok <= run * RUN - o, s, MASKED)
            s = s * TO_BASE_2
            top = jnp.maximum(m, jnp.max(s, axis=0, keepdims=True))
            e = jnp.exp2(s - top)
            exps[pl.ds(o, size), :] = e
            gws[pl.ds(o, size), :] = g
            tops[pl.ds(t * 8, 8), :] = jnp.broadcast_to(top, (8, ROWS))
            a = jnp.exp2(m - top)
            return top, l * a + jnp.sum(e, axis=0, keepdims=True), d * a + jnp.sum(e * g, axis=0, keepdims=True)

        start = (jnp.full((1, ROWS), MASKED, f32), jnp.zeros((1, ROWS), f32), jnp.zeros((1, ROWS), f32))
        carry = lax.fori_loop(0, bulk, lambda t, s: scan(t, BIG, False, s), start)
        m, l, d = lax.cond(lax.rem(small, 2) == 1, lambda: scan(bulk, BIG, True, carry), lambda: scan(bulk, SMALL, True, carry))
        share = 1.0 / l
        delta = d * share
        qg_t[...] = jnp.zeros_like(qg_t)

        def back(t, size):
            o = pl.multiple_of(t * BIG, BIG)
            span = pl.ds(o, size)
            w = exps[span, :] * (jnp.exp2(tops[pl.ds(t * 8, 8), :][:1] - m) * share)
            ds = (w * ((gws[span, :] - delta) * SCALE)).astype(bf16)
            acc[span, :LAT] += (jnp.dot(ds, qs[:, :LAT], preferred_element_type=f32)
                                + jnp.dot(w.astype(bf16), dos[...], preferred_element_type=f32))
            acc[span, LAT:] += jnp.dot(ds, qs[:, LAT:], preferred_element_type=f32)
            qg_t[...] += jnp.dot(keys_t[:KVW, span], ds, preferred_element_type=f32)

        def bulk_back(t, _):
            back(t, BIG)
            return 0

        lax.fori_loop(0, bulk, bulk_back, 0)
        pl.when(lax.rem(small, 2) == 1)(lambda: back(bulk, BIG))
        pl.when(lax.rem(small, 2) == 0)(lambda: back(bulk, SMALL))
        for h in range(0, GROUP, 2):
            a = qg_t[:, h * RUN:h * RUN + 2 * RUN].T.astype(bf16)
            qg_out[pl.ds(row, RUN), pl.ds(pl.multiple_of(half * (GROUP * KVW) + h * KVW, 128), 2 * KVW)] = jnp.concatenate([a[:RUN], a[RUN:]], axis=1)
        return 0

    lax.fori_loop(0, 4, chunk, 0)
    copy_out = pltpu.make_async_copy(qg_out, qg_ref, in_sem.at[0])
    copy_out.start()

    def leave(j, _):
        o = pl.multiple_of(j * 256, 256)
        keys[pl.ds(o, 256), :] = acc[pl.ds(o, 256), :].astype(bf16)
        for i in range(4):
            pltpu.make_async_copy(keys.at[pl.ds(o + i * RUN, RUN)], part_ref.at[chip_of[j * 4 + i]], out_sem).start()
        return 0

    lax.fori_loop(0, TOKENS // 256, leave, 0)
    pltpu.make_async_copy(keys, keys, out_sem).wait()
    copy_out.wait()


def attend(chip_run, own_run, query, out_grad, gathered):
    V, f32, bf16 = pltpu.VMEM, jnp.float32, jnp.bfloat16
    return pl.pallas_call(
        attend_kernel,
        out_shape=(jax.ShapeDtypeStruct((2 * RUN, HEADS * KVW), bf16), jax.ShapeDtypeStruct((RUNS, RUN, PAD), bf16)),
        in_specs=[pl.BlockSpec(memory_space=pltpu.SMEM)] * 2 + [pl.BlockSpec(memory_space=pl.ANY)] * 3,
        out_specs=(pl.BlockSpec(memory_space=pl.ANY),) * 2,
        scratch_shapes=[
            pltpu.SMEM((RUNS,), jnp.int32),
            V((TOKENS, PAD), bf16), V((PAD, TOKENS), bf16), V((TOKENS, PAD), f32),
            V((TOKENS, ROWS), f32), V((TOKENS, ROWS), f32), V((TOKENS // BIG * 8, ROWS), f32),
            V((ROWS, PAD), bf16), V((PAD, ROWS), bf16), V((ROWS, LAT), bf16), V((LAT, ROWS), bf16),
            V((KVW, ROWS), f32),
            V((2 * RUN, HEADS * KVW), bf16), V((2 * RUN, HEADS * LAT), bf16), V((2 * RUN, HEADS * KVW), bf16),
            pltpu.SemaphoreType.DMA, pltpu.SemaphoreType.DMA((2,)), pltpu.SemaphoreType.DMA,
        ],
        compiler_params=pltpu.CompilerParams(vmem_limit_bytes=60 * 2**20),
        cost_estimate=pl.CostEstimate(flops=46 * 10**9, bytes_accessed=2 * 10**7, transcendentals=10**7),
        name="attend",
    )(chip_run, own_run, query, out_grad, gathered)


def per_device(query, latent, out_grad, positions):
    gathered = gather(positions, latent)
    chip_run = gathered[0, :, :, :, 0, KVW].astype(jnp.int32).reshape(RUNS)
    own_run = positions[::RUN] // RUN
    query_grad, part = attend(chip_run, own_run, query, out_grad, gathered.reshape(2, RUNS, 32, PAD))
    return query_grad, scatter(part.reshape(4, 4, 4, RUN, PAD))


def solution(mesh):
    return jax.shard_map(
        per_device,
        mesh=mesh,
        in_specs=(P("seq", "tp"), P(("seq", "tp"), None), P("seq", "tp"), P("seq")),
        out_specs=(P("seq", "tp"), P(("seq", "tp"), None)),
        check_vma=False,
    )
```

time: 671 us -> 148 us (0.22)
  waiting for transfers between devices: 367 us -> 0 us
  matrix products: 169 us -> 0 us
  Pallas kernels: 0 us -> 139 us
  blocking collectives: 68.2 us -> 0 us
  other arithmetic: 40.6 us -> 2.79 us
  between operations: 13.8 us -> 0.66 us
  local copies, waits for them, and re-layouts: 12.2 us -> 4.47 us
    reduce_scatter x1 -> x0, waiting for transfers between devices: 240 us -> none  [per_device(): reduced = lax.psum_scatter(terms, 'seq', scatter_dimension=0, tiled=True)]
    dot_general x5 -> x0, matrix products: 169 us -> none  [the longest x1 59.6 us: per_device(): jnp.einsum('hij,ihd->jd', grad_scores, query_heads, preferred_element_typ...]
    pallas_call x0 -> x3, Pallas kernels: none -> 139 us  [the longest x1 76.1 us: scatter(): pl.pallas_call(functools.partial(scatter_kernel, wires), out_shape=jax.Sh...]
    all_gather x1 -> x0, waiting for transfers between devices: 126 us -> none  [per_device(): lax.all_gather(latent, ('seq', 'tp'), axis=0, tiled=True)]
    unnamed x1 -> x0, blocking collectives: 68.2 us -> none
    sub x1 -> x0, other arithmetic: 38.1 us -> none  [per_device(): exponent = jnp.exp(scores - row_top)]
  transfers between devices with their start and end apart: 3 -> 0, of which waited for: 2 -> 0; matrix products, arithmetic and copies ran while one was open for 10% -> 0% of each run, Pallas kernels for 0% -> 0%
where the time goes in v1:
time: 148 us; the launch traced here: 147 us
  Pallas kernels  139 us (94%)
  local copies, waits for them, and re-layouts  4.47 us (3%)
  other arithmetic  2.79 us (2%)
    pallas_call x1, Pallas kernels, scatter(): pl.pallas_call(functools.partial(scatter_kernel, wires), out_shape=jax.Sh...  76.1 us
    pallas_call x1, Pallas kernels, gather(): pl.pallas_call(gather_kernel, out_shape=jax.ShapeDtypeStruct((2, 4, 4, 4,...  38.8 us
    pallas_call x1, Pallas kernels, attend(): pl.pallas_call(attend_kernel, out_shape=(jax.ShapeDtypeStruct((2 * RUN, H...  24.2 us
    unnamed x3, local copies, waits for them, and re-layouts  3.12 us

profile of v1, /device:TPU:0, one launch (start us, length us, event | category | flops | bytes accessed | tf_op | source)
XLA Modules:
  0.0 147.1 jit_solution(4511837950660260733)
XLA Ops:
  0.6 0.7 slice.7
  1.4 0.6 and_select_fusion.own_run
  2.0 38.8 %gather_latent.1 = bf16[2,4,4,4,32,640]{5,4,3,2,1,0:T(8,128)(2,1)} custom-call(s32[128]{0:T(128)} %pos_ref.1, bf16[32,576]{1,0:T(8,128)(2,1)} %lat_ref.1), custom_call_target="tpu_custom_call" | custom-call | bytes 10485760 | tf_op jit(solution)/shard_map/gather_latent/pallas_call | solution.py:106
  40.8 2.2 %convert_reduce_fusion = s32[4,4,4]{2,1,0:T(4,128)S(1)} fusion(bf16[2,4,4,4,32,640]{5,4,3,2,1,0:T(8,128)(2,1)} %gather_latent.1), kind=kLoop, calls=%fused_computation | loop fusion | flops 64 | bytes 384 | tf_op jit(solution)/shard_map/convert_element_type | solution.py:396
  43.0 0.6 reshape.16.chip_run
  43.6 24.2 %attend.1 = (bf16[128,9216]{1,0:T(8,128)(2,1)}, bf16[64,64,640]{2,1,0:T(8,128)(2,1)}) custom-call(s32[64]{0:T(128)} %reshape.16.chip_run, s32[2]{0:T(128)} %and_select_fusion.own_run, bf16[128,9216]{1,0:T(8,128)(2,1)} %q_ref.1, bf16[128,8192]{1,0:T(8,128)(2,1)} %do_ref.1, bf16[2,64,32,640]{3,2,1,0:T(8,128)(2,1)} %bitcast.3), custom_call_target="tpu_custom_call" | custom-call | flops 46000001024 | bytes 20000000 | tf_op jit(solution)/shard_map/attend/pallas_call | solution.py:374
  67.8 0.0 copy-start
  67.8 2.5 %copy-done = bf16[64,64,640]{2,1,0:T(8,128)(2,1)S(1)} copy-done((bf16[64,64,640]{2,1,0:T(8,128)(2,1)S(1)}, bf16[64,64,640]{2,1,0:T(8,128)(2,1)}, u32[]{:S(2)}) %copy-start) | copy-done | bytes 5242904
  70.3 76.1 %scatter_latent_grad.1 = f32[32,576]{1,0:T(8,128)S(1)} custom-call(bf16[4,4,4,64,640]{4,3,2,1,0:T(8,128)(2,1)S(1)} %bitcast.2), custom_call_target="tpu_custom_call" | custom-call | bytes 10485760 | tf_op jit(solution)/shard_map/scatter_latent_grad/pallas_call | solution.py:233
  146.4 0.6 copy.7
Async XLA Ops:
  67.8 2.5 %copy-start = (bf16[64,64,640]{2,1,0:T(8,128)(2,1)S(1)}, bf16[64,64,640]{2,1,0:T(8,128)(2,1)}, u32[]{:S(2)}) copy-start(bf16[64,64,640]{2,1,0:T(8,128)(2,1)} %get-tuple-element.5) | copy-start | bytes 15728644

commit v2 on v1

v2 whole, which is shorter than its diff:
```python
import math

import jax, jax.numpy as jnp
from jax import lax
from jax.experimental import pallas as pl
from jax.experimental.pallas import tpu as pltpu
from jax.sharding import PartitionSpec as P

LAT=512; KVW=576; PAD=640
SCALE = 192.0 ** -0.5
TO_BASE_2 = SCALE * math.log2(math.e)
MASKED = -1e30
TOKENS = 4096
RUN = 64
RUNS = TOKENS // RUN
HEADS = 16
GROUP = 8
ROWS = GROUP * RUN
BIG, SMALL = 1024, 512
CHUNKS = 2 * HEADS // GROUP
QUARTERS = TOKENS // BIG
SLICES = CHUNKS * QUARTERS
PLAN = (4, 4, 3, 2, 1, 1, 1)
MESH = pl.DeviceIdType.MESH
PARTS = (((0, 1, 2), 0, 256), ((1, 2, 0), 256, 256), ((2, 0, 1), 512, 128))


def coords():
    seq, tp = lax.axis_index("seq"), lax.axis_index("tp")
    x = lax.rem(seq, 4)
    z = lax.rem(seq // 4, 2) * 2 + tp // 2
    y = seq // 8
    return [x, y, z], lax.rem(tp, 2)


def device(place, core):
    x, y, z = place
    return ((y * 2 + z // 2) * 4 + x, lax.rem(z, 2) * 2 + core)


def moved(place, axis, by):
    out = list(place)
    out[axis] = lax.rem(place[axis] + by, 4)
    return out


def greet(place, core, opposite=False):
    barrier = pltpu.get_barrier_semaphore()
    steps = (1, 2, 3) if opposite else (1, 3)
    for axis in range(3):
        for by in steps:
            pl.semaphore_signal(barrier, inc=1, device_id=device(moved(place, axis, by), core), device_id_type=MESH)
    pl.semaphore_signal(barrier, inc=1, device_id=device(place, 1 - core), device_id_type=MESH)
    pl.semaphore_wait(barrier, 3 * len(steps) + 1)


def gather_kernel(pos_ref, lat_ref, out_ref, own, sem, send, recv):
    place, core = coords()
    run = pos_ref[lax.rem(place[2], 2) * 64] // 64
    own[:, :KVW] = lat_ref[...]
    own[:, KVW:] = jnp.full((32, PAD - KVW), run.astype(jnp.float32)).astype(jnp.bfloat16)
    put = pltpu.make_async_copy(own, out_ref.at[core, place[0], place[1], place[2]], sem)
    put.start()
    greet(place, core, True)
    put.wait()
    sent = []

    def copy(ref, dev):
        i = len(sent)
        c = pltpu.make_async_remote_copy(ref, ref, send.at[i], recv.at[i], device_id=dev, device_id_type=MESH)
        c.start()
        sent.append(c)
        return c

    def shards(order, lane, width, at1, at2, at3, rows=(0, 32)):
        at = [None] * 3
        for axis, v in zip(order, (at1, at2, at3)):
            at[axis] = pl.ds(0, 4) if v is None else lax.rem(place[axis] + v, 4)
        return out_ref.at[core, at[0], at[1], at[2], pl.ds(*rows), pl.ds(lane, width)]

    sibling = device(place, 1 - core)
    twins = []
    one, two, three = {}, {}, {}
    steps = (1, 3, 2)

    def spread(p, d1):
        order, lane, width = PARTS[p]
        for by in steps:
            two[p, d1, by] = copy(shards(order, lane, width, d1, 0, 0), device(moved(place, order[1], by), core))

    def shift(p, d2):
        order, lane, width = PARTS[p]
        for by in (1, 3):
            three[p, d2, by] = copy(shards(order, lane, width, None, d2, 0), device(moved(place, order[2], by), core))

    def forward(p, d2):
        order, lane, width = PARTS[p]
        three[p, d2, 1].wait_recv()
        three[p, d2, 4] = copy(shards(order, lane, width, None, d2, 3, (0, 16)), device(moved(place, order[2], 1), core))
        three[p, d2, 3].wait_recv()
        three[p, d2, 5] = copy(shards(order, lane, width, None, d2, 1, (16, 16)), device(moved(place, order[2], 3), core))

    def arrive(p, d2):
        for d1 in (0, 1, 3, 2):
            two[p, d1, {3: 1, 1: 3, 2: 2}[d2]].wait_recv()

    n = range(len(PARTS))
    for p in n:
        order, lane, width = PARTS[p]
        for by in steps:
            one[p, by] = copy(shards(order, lane, width, 0, 0, 0), device(moved(place, order[0], by), core))
    for p in n:
        spread(p, 0)
    for by in steps:
        for p in n:
            one[p, by].wait_recv()
            spread(p, {1: 3, 3: 1, 2: 2}[by])
    for p in n:
        shift(p, 0)
    for d2 in (3, 1, 2):
        for p in n:
            arrive(p, d2)
            shift(p, d2)
    for p in n:
        order, lane, width = PARTS[p]
        twins.append(copy(shards(order, lane, width, None, None, 0), sibling))
    for d2 in (0, 3, 1, 2):
        for p in n:
            forward(p, d2)
    for p in n:
        order, lane, width = PARTS[p]
        twins.append(copy(shards(order, lane, width, None, None, 3), sibling))
        twins.append(copy(shards(order, lane, width, None, None, 1), sibling))
    for d2 in (0, 3, 1, 2):
        for p in n:
            order, lane, width = PARTS[p]
            three[p, d2, 4].wait_recv()
            three[p, d2, 5].wait_recv()
            twins.append(copy(shards(order, lane, width, None, d2, 2), sibling))
    for t in twins:
        t.wait_recv()
    for s in sent:
        s.wait_send()


N_GATHER = 3 * (3 + 12 + 8 + 1 + 8 + 2 + 4)


def gather(positions, latent):
    return pl.pallas_call(
        gather_kernel,
        out_shape=jax.ShapeDtypeStruct((2, 4, 4, 4, 32, PAD), jnp.bfloat16),
        in_specs=[pl.BlockSpec(memory_space=pltpu.SMEM), pl.BlockSpec(memory_space=pltpu.VMEM)],
        out_specs=pl.BlockSpec(memory_space=pl.ANY),
        scratch_shapes=[
            pltpu.VMEM((32, PAD), jnp.bfloat16),
            pltpu.SemaphoreType.DMA,
            pltpu.SemaphoreType.DMA((N_GATHER,)),
            pltpu.SemaphoreType.DMA((N_GATHER,)),
        ],
        compiler_params=pltpu.CompilerParams(collective_id=0, has_side_effects=True),
        cost_estimate=pl.CostEstimate(flops=0, bytes_accessed=10 * 2**20, transcendentals=0),
        name="gather_latent",
    )(positions, latent)


def dropped(axis, done):
    return axis - sum(1 for a in done if a < axis)


def at(ref, dim, value, rows=None):
    index = [slice(None)] * dim + [value]
    view = ref.at[tuple(index)]
    if rows is not None:
        lead = len(view.shape) - 2
        view = view.at[tuple([slice(None)] * lead + [pl.ds(*rows)])]
    return view


def scatter_kernel(part_ref, ds_ref, kt_ref, out_ref, qg_ref, mine, theirs, keep, wire, relay, landed,
                   keys_t, ds_in, qg_t, qg_out, sem, kt_sem, ds_sem, qg_sem, send, recv):
    place, core = coords()
    load_kt = pltpu.make_async_copy(kt_ref, keys_t, kt_sem)
    load_kt.start()

    def load_ds(i):
        return pltpu.make_async_copy(ds_ref.at[i // QUARTERS, pl.ds(lax.rem(i, QUARTERS) * BIG, BIG)], ds_in.at[lax.rem(i, 2)], ds_sem.at[lax.rem(i, 2)])

    load_ds(0).start()

    def slice_of_work(i, _):
        @pl.when(i + 1 < SLICES)
        def _():
            load_ds(i + 1).start()
        load_ds(i).wait()
        c, k = i // QUARTERS, lax.rem(i, QUARTERS)

        @pl.when(k == 0)
        def _():
            qg_t[...] = jnp.zeros_like(qg_t)
        qg_t[...] += jnp.dot(keys_t[:, pl.ds(pl.multiple_of(k * BIG, BIG), BIG)], ds_in[lax.rem(i, 2)], preferred_element_type=jnp.float32)

        @pl.when(k == QUARTERS - 1)
        def _():
            row = pl.multiple_of((c // 2) * RUN, RUN)
            for h in range(0, GROUP, 2):
                a = qg_t[:, h * RUN:h * RUN + 2 * RUN].T.astype(jnp.bfloat16)
                lane = pl.multiple_of(lax.rem(c, 2) * (GROUP * KVW) + h * KVW, 128)
                qg_out[pl.ds(row, RUN), pl.ds(lane, 2 * KVW)] = jnp.concatenate([a[:RUN], a[RUN:]], axis=1)
        return 0

    done_work = [0]

    def work(n):
        first = done_work[0]
        done_work[0] += n
        lax.fori_loop(first, first + n, slice_of_work, 0)

    greet(place, core)
    count = [0]
    sent = []

    def copy(src, dst, dev):
        i = count[0]
        count[0] += 1
        c = pltpu.make_async_remote_copy(src, dst, send.at[i], recv.at[i], device_id=dev, device_id_type=MESH)
        c.start()
        sent.append(c)
        return c

    sibling = device(place, 1 - core)
    swaps, loads = [], []
    for n, (order, lane, width) in enumerate(PARTS):
        other = part_ref.at[:, :, :, pl.ds(32 * (1 - core), 32), pl.ds(lane, width)]
        swaps.append(copy(other, theirs[n], sibling))
        load = pltpu.make_async_copy(part_ref.at[:, :, :, pl.ds(32 * core, 32), pl.ds(lane, width)], mine[n], sem.at[n])
        load.start()
        loads.append(load)

    load_kt.wait()
    work(PLAN[0])
    halves = ((0, 16), (16, 16))
    for phase in range(3):
        started = []
        for n, (order, lane, width) in enumerate(PARTS):
            axis, done = order[phase], order[:phase]
            dim = dropped(axis, done)
            k, w, rl, ld = keep[n][phase], wire[n][phase], relay[n][phase], landed[n][phase]
            me = place[axis]
            right, left, opp = (lax.rem(me + i, 4) for i in (1, 3, 2))
            rdev, ldev = device(moved(place, axis, 1), core), device(moved(place, axis, 3), core)
            if phase == 0:
                loads[n].wait()
                swaps[n].wait_recv()
                def fill(v):
                    at(k, dim, v)[...] = at(mine[n], dim, v)[...].astype(jnp.float32) + at(theirs[n], dim, v)[...].astype(jnp.float32)
            else:
                def fill(v):
                    pass
            fill(opp)
            at(w, dim, opp)[...] = at(k, dim, opp)[...].astype(w.dtype)
            c0 = copy(at(w, dim, opp, halves[0]), rl.at[0], rdev)
            c1 = copy(at(w, dim, opp, halves[1]), rl.at[1], ldev)
            fill(right)
            at(w, dim, right, halves[1])[...] = at(k, dim, right, halves[1])[...].astype(w.dtype)
            c2 = copy(at(w, dim, right, halves[1]), ld.at[0, 1], rdev)
            fill(left)
            at(w, dim, left, halves[0])[...] = at(k, dim, left, halves[0])[...].astype(w.dtype)
            c3 = copy(at(w, dim, left, halves[0]), ld.at[1, 0], ldev)
            fill(me)
            started.append((c0, c1, c2, c3))
        work(PLAN[1 + 2 * phase])
        ended = []
        for n, (order, lane, width) in enumerate(PARTS):
            axis, done = order[phase], order[:phase]
            dim = dropped(axis, done)
            k, w, rl, ld = keep[n][phase], wire[n][phase], relay[n][phase], landed[n][phase]
            me = place[axis]
            right, left = lax.rem(me + 1, 4), lax.rem(me + 3, 4)
            rdev, ldev = device(moved(place, axis, 1), core), device(moved(place, axis, 3), core)
            c0, c1, c2, c3 = started[n]
            c0.wait_recv()
            at(w, dim, right, halves[0])[...] = (at(k, dim, right, halves[0])[...] + rl[0].astype(jnp.float32)).astype(w.dtype)
            c4 = copy(at(w, dim, right, halves[0]), ld.at[0, 0], rdev)
            c1.wait_recv()
            at(w, dim, left, halves[1])[...] = (at(k, dim, left, halves[1])[...] + rl[1].astype(jnp.float32)).astype(w.dtype)
            c5 = copy(at(w, dim, left, halves[1]), ld.at[1, 1], ldev)
            ended.append((c2, c3, c4, c5))
        work(PLAN[2 + 2 * phase])
        if phase == 2:
            put = pltpu.make_async_copy(qg_out, qg_ref, qg_sem)
            put.start()
        for n, (order, lane, width) in enumerate(PARTS):
            axis, done = order[phase], order[:phase]
            dim = dropped(axis, done)
            k, ld = keep[n][phase], landed[n][phase]
            for c in ended[n]:
                c.wait_recv()
            for h in (0, 1):
                total = (at(k, dim, place[axis], halves[h])[...] + ld[0, h].astype(jnp.float32)) + ld[1, h].astype(jnp.float32)
                if phase < 2:
                    to = keep[n][phase + 1]
                    to.at[tuple([slice(None)] * (2 - phase) + [pl.ds(*halves[h])])][...] = total
                else:
                    real = min(width, KVW - lane)
                    out_ref[pl.ds(*halves[h]), pl.ds(lane, real)] = total[:, :real]
    put.wait()
    for s in sent:
        s.wait_send()


N_SCATTER = 3 + 9 * 6
WIRES = (jnp.bfloat16, jnp.float32, jnp.float32)


def scatter(part, ds, keys_t):
    V, f32, bf16 = pltpu.VMEM, jnp.float32, jnp.bfloat16
    mine = [V((4, 4, 4, 32, w), bf16) for _, _, w in PARTS]
    keep = [[V((4,) * (3 - p) + (32, w), f32) for p in range(3)] for _, _, w in PARTS]
    wire = [[V((4,) * (3 - p) + (32, w), WIRES[p]) for p in range(3)] for _, _, w in PARTS]
    relay = [[V((2,) + (4,) * (2 - p) + (16, w), WIRES[p]) for p in range(3)] for _, _, w in PARTS]
    landed = [[V((2, 2) + (4,) * (2 - p) + (16, w), WIRES[p]) for p in range(3)] for _, _, w in PARTS]
    return pl.pallas_call(
        scatter_kernel,
        out_shape=(jax.ShapeDtypeStruct((32, KVW), f32), jax.ShapeDtypeStruct((2 * RUN, HEADS * KVW), bf16)),
        in_specs=[pl.BlockSpec(memory_space=pltpu.HBM)] * 3,
        out_specs=(pl.BlockSpec(memory_space=pltpu.VMEM), pl.BlockSpec(memory_space=pltpu.HBM)),
        scratch_shapes=[
            mine, list(mine), keep, wire, relay, landed,
            V((KVW, TOKENS), bf16), V((2, BIG, ROWS), bf16), V((KVW, ROWS), f32), V((2 * RUN, HEADS * KVW), bf16),
            pltpu.SemaphoreType.DMA((3,)), pltpu.SemaphoreType.DMA, pltpu.SemaphoreType.DMA((2,)), pltpu.SemaphoreType.DMA,
            pltpu.SemaphoreType.DMA((N_SCATTER,)),
            pltpu.SemaphoreType.DMA((N_SCATTER,)),
        ],
        compiler_params=pltpu.CompilerParams(collective_id=1, has_side_effects=True, vmem_limit_bytes=56 * 2**20),
        cost_estimate=pl.CostEstimate(flops=10**10, bytes_accessed=3 * 10**7, transcendentals=0),
        name="scatter_latent_grad",
    )(part, ds, keys_t)


def attend_kernel(pos_ref, q_ref, do_ref, kg_ref, ds_ref, kt_ref, part_ref,
                  chip_run, chip_of, keys, keys_t, acc, exps, gws, tops, qs, qs_t, dos, dos_t, q_in, do_in, ds_out, zeros,
                  tags, tags_i, key_sem, in_sem, out_sem, ds_sem, zero_sem):
    f32, bf16 = jnp.float32, jnp.bfloat16
    copy_q = pltpu.make_async_copy(q_ref, q_in, in_sem.at[0])
    copy_do = pltpu.make_async_copy(do_ref, do_in, in_sem.at[1])
    copy_tags = pltpu.make_async_copy(kg_ref.at[0, :, pl.ds(0, 16), pl.ds(LAT, 128)], tags, in_sem.at[2])
    copy_tags.start()
    copy_q.start()
    copy_do.start()
    zeros[...] = jnp.zeros_like(zeros)
    copy_tags.wait()
    tags_i[...] = tags[:, 0, :].astype(f32).astype(jnp.int32)
    move_tags = pltpu.make_async_copy(tags_i, chip_run, in_sem.at[2])
    move_tags.start()
    acc[...] = jnp.zeros_like(acc)
    move_tags.wait()

    def place(chip, _):
        run = chip_run[chip, KVW - LAT]
        chip_of[run] = chip
        for c in range(2):
            pltpu.make_async_copy(kg_ref.at[c, chip], keys.at[pl.ds(run * RUN + c * 32, 32)], key_sem).start()
        return 0

    lax.fori_loop(0, RUNS, place, 0)
    qs[:, LAT:] = jnp.zeros((ROWS, PAD - LAT), bf16)
    pltpu.make_async_copy(keys, keys, key_sem).wait()

    def turn(j, _):
        o = pl.multiple_of(j * 256, 256)
        keys_t[:, pl.ds(o, 256)] = keys[pl.ds(o, 256), :KVW].T
        return 0

    lax.fori_loop(0, TOKENS // 256, turn, 0)
    copy_kt = pltpu.make_async_copy(keys_t, kt_ref, in_sem.at[2])
    copy_kt.start()
    copy_q.wait()
    copy_do.wait()

    def chunk(c, made):
        half, block = lax.rem(c, 2), c // 2
        run = pos_ref[block * RUN] // RUN
        row = pl.multiple_of(block * RUN, RUN)
        for h in range(0, GROUP, 2):
            v = q_in[pl.ds(row, RUN), pl.ds(pl.multiple_of(half * (GROUP * KVW) + h * KVW, 128), 2 * KVW)]
            qs[h * RUN:h * RUN + RUN, :KVW] = v[:, :KVW]
            qs[h * RUN + RUN:h * RUN + 2 * RUN, :KVW] = v[:, KVW:]
            d = do_in[pl.ds(row, RUN), pl.ds(pl.multiple_of(half * (GROUP * LAT) + h * LAT, 128), 2 * LAT)]
            dos[h * RUN:h * RUN + RUN, :] = d[:, :LAT]
            dos[h * RUN + RUN:h * RUN + 2 * RUN, :] = d[:, LAT:]
        qs_t[...] = qs[...].T
        dos_t[...] = dos[...].T
        small = run // (SMALL // RUN)
        bulk = small // 2
        odd = lax.rem(small, 2) == 1

        def scan(t, size, masked, carry):
            m, l, d = carry
            o = pl.multiple_of(t * BIG, BIG)
            tile = keys[pl.ds(o, size), :]
            s = jnp.dot(tile, qs_t[...], preferred_element_type=f32)
            g = jnp.dot(tile[:, :LAT], dos_t[...], preferred_element_type=f32)
            if masked:
                key = lax.broadcasted_iota(jnp.int32, (size, ROWS), 0)
                tok = lax.broadcasted_iota(jnp.int32, (size, ROWS), 1) % RUN
                s = jnp.where(key - tok <= run * RUN - o, s, MASKED)
            s = s * TO_BASE_2
            top = jnp.maximum(m, jnp.max(s, axis=0, keepdims=True))
            e = jnp.exp2(s - top)
            exps[pl.ds(o, size), :] = e
            gws[pl.ds(o, size), :] = g
            tops[pl.ds(t * 8, 8), :] = jnp.broadcast_to(top, (8, ROWS))
            a = jnp.exp2(m - top)
            return top, l * a + jnp.sum(e, axis=0, keepdims=True), d * a + jnp.sum(e * g, axis=0, keepdims=True)

        start = (jnp.full((1, ROWS), MASKED, f32), jnp.zeros((1, ROWS), f32), jnp.zeros((1, ROWS), f32))
        carry = lax.fori_loop(0, bulk, lambda t, s: scan(t, BIG, False, s), start)
        m, l, d = lax.cond(odd, lambda: scan(bulk, BIG, True, carry), lambda: scan(bulk, SMALL, True, carry))
        share = 1.0 / l
        delta = d * share

        def leave_ds(slot, t):
            return pltpu.make_async_copy(ds_out.at[slot], ds_ref.at[c, pl.ds(t * BIG, BIG)], ds_sem.at[slot])

        def back(t, size):
            n = made + t
            slot = lax.rem(n, 2)

            @pl.when(n >= 2)
            def _():
                leave_ds(slot, t).wait()
            o = pl.multiple_of(t * BIG, BIG)
            span = pl.ds(o, size)
            w = exps[span, :] * (jnp.exp2(tops[pl.ds(t * 8, 8), :][:1] - m) * share)
            ds = (w * ((gws[span, :] - delta) * SCALE)).astype(bf16)
            ds_out[slot, :size] = ds
            if size < BIG:
                ds_out[slot, size:] = jnp.zeros((BIG - size, ROWS), bf16)
            leave_ds(slot, t).start()
            nt = (((1,), (1,)), ((), ()))
            acc[:LAT, span] += (lax.dot_general(qs_t[:LAT], ds, nt, preferred_element_type=f32)
                                + lax.dot_general(dos_t[...], w.astype(bf16), nt, preferred_element_type=f32))
            acc[LAT:, span] += lax.dot_general(qs_t[LAT:KVW], ds, nt, preferred_element_type=f32)

        def bulk_back(t, _):
            back(t, BIG)
            return 0

        lax.fori_loop(0, bulk, bulk_back, 0)
        pl.when(odd)(lambda: back(bulk, BIG))
        pl.when(jnp.logical_not(odd))(lambda: back(bulk, SMALL))

        def blank(t, _):
            pltpu.make_async_copy(zeros, ds_ref.at[c, pl.ds(t * BIG, BIG)], zero_sem).start()
            return 0

        lax.fori_loop(bulk + 1, QUARTERS, blank, 0)
        return made + bulk + 1

    made = lax.fori_loop(0, CHUNKS, chunk, 0)

    def leave(j, _):
        o = pl.multiple_of(j * 256, 256)
        keys[pl.ds(o, 256), :KVW] = acc[:, pl.ds(o, 256)].astype(bf16).T
        for i in range(4):
            pltpu.make_async_copy(keys.at[pl.ds(o + i * RUN, RUN)], part_ref.at[chip_of[j * 4 + i]], out_sem).start()
        return 0

    lax.fori_loop(0, TOKENS // 256, leave, 0)
    copy_kt.wait()
    for slot in range(2):
        pltpu.make_async_copy(ds_out.at[slot], ds_ref.at[0, pl.ds(0, BIG)], ds_sem.at[slot]).wait()

    def blanked(i, _):
        pltpu.make_async_copy(zeros, ds_ref.at[0, pl.ds(0, BIG)], zero_sem).wait()
        return 0

    lax.fori_loop(made, SLICES, blanked, 0)
    pltpu.make_async_copy(keys, keys, out_sem).wait()


def attend(positions, query, out_grad, gathered):
    V, f32, bf16 = pltpu.VMEM, jnp.float32, jnp.bfloat16
    return pl.pallas_call(
        attend_kernel,
        out_shape=(jax.ShapeDtypeStruct((CHUNKS, TOKENS, ROWS), bf16), jax.ShapeDtypeStruct((KVW, TOKENS), bf16),
                   jax.ShapeDtypeStruct((RUNS, RUN, PAD), bf16)),
        in_specs=[pl.BlockSpec(memory_space=pltpu.SMEM)] + [pl.BlockSpec(memory_space=pltpu.HBM)] * 3,
        out_specs=(pl.BlockSpec(memory_space=pltpu.HBM),) * 3,
        scratch_shapes=[
            pltpu.SMEM((RUNS, 128), jnp.int32), pltpu.SMEM((RUNS,), jnp.int32),
            V((TOKENS, PAD), bf16), V((KVW, TOKENS), bf16), V((KVW, TOKENS), f32),
            V((TOKENS, ROWS), f32), V((TOKENS, ROWS), f32), V((QUARTERS * 8, ROWS), f32),
            V((ROWS, PAD), bf16), V((PAD, ROWS), bf16), V((ROWS, LAT), bf16), V((LAT, ROWS), bf16),
            V((2 * RUN, HEADS * KVW), bf16), V((2 * RUN, HEADS * LAT), bf16), V((2, BIG, ROWS), bf16), V((BIG, ROWS), bf16),
            V((RUNS, 16, 128), bf16), V((RUNS, 128), jnp.int32),
            pltpu.SemaphoreType.DMA, pltpu.SemaphoreType.DMA((3,)), pltpu.SemaphoreType.DMA, pltpu.SemaphoreType.DMA((2,)),
            pltpu.SemaphoreType.DMA,
        ],
        compiler_params=pltpu.CompilerParams(vmem_limit_bytes=60 * 2**20),
        cost_estimate=pl.CostEstimate(flops=46 * 10**9, bytes_accessed=2 * 10**7, transcendentals=10**7),
        name="attend",
    )(positions, query, out_grad, gathered)


def per_device(query, latent, out_grad, positions):
    gathered = gather(positions, latent)
    ds, keys_t, part = attend(positions, query, out_grad, gathered.reshape(2, RUNS, 32, PAD))
    latent_grad, query_grad = scatter(part.reshape(4, 4, 4, RUN, PAD), ds, keys_t)
    return query_grad, latent_grad


def solution(mesh):
    return jax.shard_map(
        per_device,
        mesh=mesh,
        in_specs=(P("seq", "tp"), P(("seq", "tp"), None), P("seq", "tp"), P("seq")),
        out_specs=(P("seq", "tp"), P(("seq", "tp"), None)),
        check_vma=False,
    )
```

time: 148 us -> 130 us (0.88)
  Pallas kernels: 139 us -> 125 us
  other arithmetic: 2.79 us -> 0 us
    pallas_call x1, Pallas kernels: 38.8 us -> 29.4 us  [gather(): pl.pallas_call(gather_kernel, out_shape=jax.ShapeDtypeStruct((2, 4, 4, 4,...]
    pallas_call x2, Pallas kernels: 100 us -> 95.6 us  [the longest x1 53.3 us: scatter(): pl.pallas_call(scatter_kernel, out_shape=(jax.ShapeDtypeStruct((32, KVW),...]
    convert_element_type x1 -> x0, other arithmetic: 2.21 us -> none  [per_device(): chip_run = gathered[0, :, :, :, 0, KVW].astype(jnp.int32).reshape(RUNS)]
    unnamed x3 -> x4, local copies, waits for them, and re-layouts: 3.12 us -> 3.89 us
where the time goes in v2:
time: 130 us
  Pallas kernels  125 us (96%)
  local copies, waits for them, and re-layouts  3.89 us (3%)
    pallas_call x1, Pallas kernels, scatter(): pl.pallas_call(scatter_kernel, out_shape=(jax.ShapeDtypeStruct((32, KVW),...  53.3 us
    pallas_call x1, Pallas kernels, attend(): pl.pallas_call(attend_kernel, out_shape=(jax.ShapeDtypeStruct((CHUNKS, TO...  42.3 us
    pallas_call x1, Pallas kernels, gather(): pl.pallas_call(gather_kernel, out_shape=jax.ShapeDtypeStruct((2, 4, 4, 4,...  29.4 us
    unnamed x4, local copies, waits for them, and re-layouts  3.89 us

profile of v2, /device:TPU:0, one launch (start us, length us, event | category | flops | bytes accessed | tf_op | source)
XLA Modules:
  0.0 129.6 jit_solution(11559913218267380547)
XLA Ops:
  0.6 29.4 %gather_latent.1 = bf16[2,4,4,4,32,640]{5,4,3,2,1,0:T(8,128)(2,1)} custom-call(s32[128]{0:T(128)} %pos_ref.3, bf16[32,576]{1,0:T(8,128)(2,1)} %lat_ref.1), custom_call_target="tpu_custom_call" | custom-call | bytes 10485760 | tf_op jit(solution)/shard_map/gather_latent/pallas_call | solution.py:150
  30.1 42.3 %attend.1 = (bf16[4,4096,512]{2,1,0:T(8,128)(2,1)}, bf16[576,4096]{1,0:T(8,128)(2,1)}, bf16[64,64,640]{2,1,0:T(8,128)(2,1)}) custom-call(s32[128]{0:T(128)} %pos_ref.3, bf16[128,9216]{1,0:T(8,128)(2,1)} %q_ref.1, bf16[128,8192]{1,0:T(8,128)(2,1)} %do_ref.1, bf16[2,64,32,640]{3,2,1,0:T(8,128)(2,1)} %bitcast.2), custom_call_target="tpu_custom_call" | custom-call | flops 46000001024 | bytes 20000000 | tf_op jit(solution)/shard_map/attend/pallas_call | solution.py:485
  72.4 53.3 %scatter_latent_grad.1 = (f32[32,576]{1,0:T(8,128)}, bf16[128,9216]{1,0:T(8,128)(2,1)}) custom-call(bf16[4,4,4,64,640]{4,3,2,1,0:T(8,128)(2,1)} %bitcast.3, bf16[4,4096,512]{2,1,0:T(8,128)(2,1)} %get-tuple-element.8.ds_ref, bf16[576,4096]{1,0:T(8,128)(2,1)} %get-tuple-element.9.kt_ref), custom_call_target="tpu_custom_call" | custom-call | flops 10000000000 | bytes 30000000 | tf_op jit(solution)/shard_map/scatter_latent_grad/pallas_call | solution.py:323
  125.7 0.0 copy-start
  125.7 3.3 %copy.8 = bf16[128,9216]{1,0:T(8,128)(2,1)} copy(bf16[128,9216]{1,0:T(8,128)(2,1)} %get-tuple-element.14) | data formatting | bytes 4718592
  129.0 0.0 copy-done
  129.0 0.6 copy.9
Async XLA Ops:
  125.7 3.3 %copy-start = (f32[32,576]{1,0:T(8,128)S(1)}, f32[32,576]{1,0:T(8,128)}, u32[]{:S(2)}) copy-start(f32[32,576]{1,0:T(8,128)} %get-tuple-element.15) | copy-start | bytes 221188

commit v3 on v2

--- a/solution.py
+++ b/solution.py
@@ -16,7 +16,7 @@
 HEADS = 16
 GROUP = 8
 ROWS = GROUP * RUN
-BIG, SMALL = 1024, 512
+HUGE, BIG, SMALL = 2048, 1024, 512
 CHUNKS = 2 * HEADS // GROUP
 QUARTERS = TOKENS // BIG
 SLICES = CHUNKS * QUARTERS
@@ -54,12 +54,12 @@
     pl.semaphore_wait(barrier, 3 * len(steps) + 1)
 
 
-def gather_kernel(pos_ref, lat_ref, out_ref, own, sem, send, recv):
+def gather_kernel(pos_ref, lat_ref, out_ref, runs_ref, own, tags, tags_f, sem, send, recv):
     place, core = coords()
     run = pos_ref[lax.rem(place[2], 2) * 64] // 64
     own[:, :KVW] = lat_ref[...]
     own[:, KVW:] = jnp.full((32, PAD - KVW), run.astype(jnp.float32)).astype(jnp.bfloat16)
-    put = pltpu.make_async_copy(own, out_ref.at[core, place[0], place[1], place[2]], sem)
+    put = pltpu.make_async_copy(own, out_ref.at[place[0], place[1], place[2], core], sem)
     put.start()
     greet(place, core, True)
     put.wait()
@@ -76,7 +76,7 @@
         at = [None] * 3
         for axis, v in zip(order, (at1, at2, at3)):
             at[axis] = pl.ds(0, 4) if v is None else lax.rem(place[axis] + v, 4)
-        return out_ref.at[core, at[0], at[1], at[2], pl.ds(*rows), pl.ds(lane, width)]
+        return out_ref.at[at[0], at[1], at[2], core, pl.ds(*rows), pl.ds(lane, width)]
 
     sibling = device(place, 1 - core)
     twins = []
@@ -131,12 +131,19 @@
         order, lane, width = PARTS[p]
         twins.append(copy(shards(order, lane, width, None, None, 3), sibling))
         twins.append(copy(shards(order, lane, width, None, None, 1), sibling))
-    for d2 in (0, 3, 1, 2):
-        for p in n:
-            order, lane, width = PARTS[p]
+    for p in (2, 0, 1):
+        order, lane, width = PARTS[p]
+        for d2 in (0, 3, 1, 2):
             three[p, d2, 4].wait_recv()
             three[p, d2, 5].wait_recv()
             twins.append(copy(shards(order, lane, width, None, d2, 2), sibling))
+        if p == 2:
+            load_tags = pltpu.make_async_copy(out_ref.at[:, :, :, core, pl.ds(0, 16), pl.ds(LAT, 128)], tags, sem)
+            load_tags.start()
+    load_tags.wait()
+    tags_f[...] = jnp.zeros_like(tags_f)
+    tags_f[:RUNS, :] = tags[:, :, :, 0, :].reshape(RUNS, 128).astype(jnp.float32)
+    runs_ref[...] = tags_f[...].T[KVW - LAT:KVW - LAT + 8, :].astype(jnp.int32)
     for t in twins:
         t.wait_recv()
     for s in sent:
@@ -149,11 +156,13 @@
 def gather(positions, latent):
     return pl.pallas_call(
         gather_kernel,
-        out_shape=jax.ShapeDtypeStruct((2, 4, 4, 4, 32, PAD), jnp.bfloat16),
+        out_shape=(jax.ShapeDtypeStruct((4, 4, 4, 2, 32, PAD), jnp.bfloat16), jax.ShapeDtypeStruct((8, 128), jnp.int32)),
         in_specs=[pl.BlockSpec(memory_space=pltpu.SMEM), pl.BlockSpec(memory_space=pltpu.VMEM)],
-        out_specs=pl.BlockSpec(memory_space=pl.ANY),
+        out_specs=(pl.BlockSpec(memory_space=pltpu.HBM), pl.BlockSpec(memory_space=pltpu.VMEM)),
         scratch_shapes=[
             pltpu.VMEM((32, PAD), jnp.bfloat16),
+            pltpu.VMEM((4, 4, 4, 16, 128), jnp.bfloat16),
+            pltpu.VMEM((128, 128), jnp.float32),
             pltpu.SemaphoreType.DMA,
             pltpu.SemaphoreType.DMA((N_GATHER,)),
             pltpu.SemaphoreType.DMA((N_GATHER,)),
@@ -177,11 +186,11 @@
     return view
 
 
-def scatter_kernel(part_ref, ds_ref, kt_ref, out_ref, qg_ref, mine, theirs, keep, wire, relay, landed,
-                   keys_t, ds_in, qg_t, qg_out, sem, kt_sem, ds_sem, qg_sem, send, recv):
+def scatter_kernel(part_ref, ds_ref, keys_ref, out_ref, qg_ref, mine, theirs, keep, wire, relay, landed,
+                   keys, keys_t, ds_in, qg_t, qg_out, sem, kt_sem, ds_sem, qg_sem, send, recv):
     place, core = coords()
-    load_kt = pltpu.make_async_copy(kt_ref, keys_t, kt_sem)
-    load_kt.start()
+    load_keys = pltpu.make_async_copy(keys_ref, keys, kt_sem)
+    load_keys.start()
 
     def load_ds(i):
         return pltpu.make_async_copy(ds_ref.at[i // QUARTERS, pl.ds(lax.rem(i, QUARTERS) * BIG, BIG)], ds_in.at[lax.rem(i, 2)], ds_sem.at[lax.rem(i, 2)])
@@ -237,7 +246,14 @@
         load.start()
         loads.append(load)
 
-    load_kt.wait()
+    load_keys.wait()
+
+    def turn(j, _):
+        o = pl.multiple_of(j * 256, 256)
+        keys_t[:, pl.ds(o, 256)] = keys[pl.ds(o, 256), :KVW].T
+        return 0
+
+    lax.fori_loop(0, TOKENS // 256, turn, 0)
     work(PLAN[0])
     halves = ((0, 16), (16, 16))
     for phase in range(3):
@@ -313,7 +329,7 @@
 WIRES = (jnp.bfloat16, jnp.float32, jnp.float32)
 
 
-def scatter(part, ds, keys_t):
+def scatter(part, ds, keys):
     V, f32, bf16 = pltpu.VMEM, jnp.float32, jnp.bfloat16
     mine = [V((4, 4, 4, 32, w), bf16) for _, _, w in PARTS]
     keep = [[V((4,) * (3 - p) + (32, w), f32) for p in range(3)] for _, _, w in PARTS]
@@ -327,7 +343,7 @@
         out_specs=(pl.BlockSpec(memory_space=pltpu.VMEM), pl.BlockSpec(memory_space=pltpu.HBM)),
         scratch_shapes=[
             mine, list(mine), keep, wire, relay, landed,
-            V((KVW, TOKENS), bf16), V((2, BIG, ROWS), bf16), V((KVW, ROWS), f32), V((2 * RUN, HEADS * KVW), bf16),
+            V((TOKENS, PAD), bf16), V((KVW, TOKENS), bf16), V((2, BIG, ROWS), bf16), V((KVW, ROWS), f32), V((2 * RUN, HEADS * KVW), bf16),
             pltpu.SemaphoreType.DMA((3,)), pltpu.SemaphoreType.DMA, pltpu.SemaphoreType.DMA((2,)), pltpu.SemaphoreType.DMA,
             pltpu.SemaphoreType.DMA((N_SCATTER,)),
             pltpu.SemaphoreType.DMA((N_SCATTER,)),
@@ -335,51 +351,56 @@
         compiler_params=pltpu.CompilerParams(collective_id=1, has_side_effects=True, vmem_limit_bytes=56 * 2**20),
         cost_estimate=pl.CostEstimate(flops=10**10, bytes_accessed=3 * 10**7, transcendentals=0),
         name="scatter_latent_grad",
-    )(part, ds, keys_t)
-
-
-def attend_kernel(pos_ref, q_ref, do_ref, kg_ref, ds_ref, kt_ref, part_ref,
-                  chip_run, chip_of, keys, keys_t, acc, exps, gws, tops, qs, qs_t, dos, dos_t, q_in, do_in, ds_out, zeros,
-                  tags, tags_i, key_sem, in_sem, out_sem, ds_sem, zero_sem):
+    )(part, ds, keys)
+
+
+def attend_kernel(pos_ref, runs_ref, q_ref, do_ref, kg_ref, ds_ref, keys_ref, part_ref,
+                  chip_of, keys, acc, exps, gws, tops, qs, qs_t, dos, dos_t, q_in, do_in, ds_out,
+                  key_sem, in_sem, out_sem, ds_sem):
     f32, bf16 = jnp.float32, jnp.bfloat16
-    copy_q = pltpu.make_async_copy(q_ref, q_in, in_sem.at[0])
-    copy_do = pltpu.make_async_copy(do_ref, do_in, in_sem.at[1])
-    copy_tags = pltpu.make_async_copy(kg_ref.at[0, :, pl.ds(0, 16), pl.ds(LAT, 128)], tags, in_sem.at[2])
-    copy_tags.start()
-    copy_q.start()
-    copy_do.start()
-    zeros[...] = jnp.zeros_like(zeros)
-    copy_tags.wait()
-    tags_i[...] = tags[:, 0, :].astype(f32).astype(jnp.int32)
-    move_tags = pltpu.make_async_copy(tags_i, chip_run, in_sem.at[2])
-    move_tags.start()
+    copy_keys = pltpu.make_async_copy(keys, keys_ref, out_sem.at[1])
+
+    def inputs(c):
+        row = pl.ds(pl.multiple_of((c // 2) * RUN, RUN), RUN)
+        out = []
+        for i, (ref, to, width) in enumerate(((q_ref, q_in, GROUP * KVW), (do_ref, do_in, GROUP * LAT))):
+            lane = pl.ds(pl.multiple_of(lax.rem(c, 2) * width, 128), width)
+            out.append(pltpu.make_async_copy(ref.at[row, lane], to.at[row, lane], in_sem.at[i, c]))
+        return out
+
+    def take(c, _):
+        for copy in inputs(c):
+            copy.start()
+        return 0
+
+    take(0, 0)
+
+    def place(chip, _):
+        chip_of[runs_ref[0, chip]] = chip
+        return 0
+
+    lax.fori_loop(0, RUNS, place, 0)
+
+    def fetch(j, _):
+        pltpu.make_async_copy(kg_ref.at[chip_of[j]], keys.at[pl.ds(j * RUN, RUN)], key_sem.at[j // (BIG // RUN)]).start()
+        return 0
+
+    lax.fori_loop(0, BIG // RUN, fetch, 0)
+    lax.fori_loop(BIG // RUN, RUNS, fetch, 0)
+    lax.fori_loop(1, CHUNKS, take, 0)
+
+    def await_keys(t, _):
+        tile = keys.at[pl.ds(pl.multiple_of(t * BIG, BIG), BIG)]
+        pltpu.make_async_copy(tile, tile, key_sem.at[t]).wait()
+        return 0
+
     acc[...] = jnp.zeros_like(acc)
-    move_tags.wait()
-
-    def place(chip, _):
-        run = chip_run[chip, KVW - LAT]
-        chip_of[run] = chip
-        for c in range(2):
-            pltpu.make_async_copy(kg_ref.at[c, chip], keys.at[pl.ds(run * RUN + c * 32, 32)], key_sem).start()
-        return 0
-
-    lax.fori_loop(0, RUNS, place, 0)
     qs[:, LAT:] = jnp.zeros((ROWS, PAD - LAT), bf16)
-    pltpu.make_async_copy(keys, keys, key_sem).wait()
-
-    def turn(j, _):
-        o = pl.multiple_of(j * 256, 256)
-        keys_t[:, pl.ds(o, 256)] = keys[pl.ds(o, 256), :KVW].T
-        return 0
-
-    lax.fori_loop(0, TOKENS // 256, turn, 0)
-    copy_kt = pltpu.make_async_copy(keys_t, kt_ref, in_sem.at[2])
-    copy_kt.start()
-    copy_q.wait()
-    copy_do.wait()
-
-    def chunk(c, made):
-        half, block = lax.rem(c, 2), c // 2
+
+    def chunk(c, _):
+        for copy in inputs(c):
+            copy.wait()
+        half, block, slot = lax.rem(c, 2), c // 2, lax.rem(c, 2)
         run = pos_ref[block * RUN] // RUN
         row = pl.multiple_of(block * RUN, RUN)
         for h in range(0, GROUP, 2):
@@ -391,13 +412,21 @@
             dos[h * RUN + RUN:h * RUN + 2 * RUN, :] = d[:, LAT:]
         qs_t[...] = qs[...].T
         dos_t[...] = dos[...].T
-        small = run // (SMALL // RUN)
-        bulk = small // 2
-        odd = lax.rem(small, 2) == 1
-
-        def scan(t, size, masked, carry):
+        full = run // (SMALL // RUN)
+        huge = full // 4
+        rest = lax.rem(full, 4)
+        big = rest // 2
+        odd = lax.rem(rest, 2) == 1
+        last = huge * 4 + big * 2
+
+        def scan(u, size, masked, carry):
             m, l, d = carry
-            o = pl.multiple_of(t * BIG, BIG)
+
+            @pl.when(c == 0)
+            def _():
+                for i in range(max(size // BIG, 1)):
+                    await_keys(u // 2 + i, 0)
+            o = pl.multiple_of(u * SMALL, SMALL)
             tile = keys[pl.ds(o, size), :]
             s = jnp.dot(tile, qs_t[...], preferred_element_type=f32)
             g = jnp.dot(tile[:, :LAT], dos_t[...], preferred_element_type=f32)
@@ -410,105 +439,127 @@
             e = jnp.exp2(s - top)
             exps[pl.ds(o, size), :] = e
             gws[pl.ds(o, size), :] = g
-            tops[pl.ds(t * 8, 8), :] = jnp.broadcast_to(top, (8, ROWS))
+            tops[pl.ds(pl.multiple_of(u * 8, 8), 8), :] = jnp.broadcast_to(top, (8, ROWS))
             a = jnp.exp2(m - top)
             return top, l * a + jnp.sum(e, axis=0, keepdims=True), d * a + jnp.sum(e * g, axis=0, keepdims=True)
 
         start = (jnp.full((1, ROWS), MASKED, f32), jnp.zeros((1, ROWS), f32), jnp.zeros((1, ROWS), f32))
-        carry = lax.fori_loop(0, bulk, lambda t, s: scan(t, BIG, False, s), start)
-        m, l, d = lax.cond(odd, lambda: scan(bulk, BIG, True, carry), lambda: scan(bulk, SMALL, True, carry))
+        carry = lax.fori_loop(0, huge, lambda t, s: scan(t * 4, HUGE, False, s), start)
+        carry = lax.fori_loop(0, big, lambda t, s: scan(huge * 4, BIG, False, s), carry)
+        m, l, d = lax.cond(odd, lambda: scan(last, BIG, True, carry), lambda: scan(last, SMALL, True, carry))
+
+        @pl.when(c == 0)
+        def _():
+            lax.fori_loop(last // 2 + 1, TOKENS // BIG, await_keys, 0)
+            copy_keys.start()
         share = 1.0 / l
         delta = d * share
 
-        def leave_ds(slot, t):
-            return pltpu.make_async_copy(ds_out.at[slot], ds_ref.at[c, pl.ds(t * BIG, BIG)], ds_sem.at[slot])
-
-        def back(t, size):
-            n = made + t
-            slot = lax.rem(n, 2)
-
-            @pl.when(n >= 2)
-            def _():
-                leave_ds(slot, t).wait()
-            o = pl.multiple_of(t * BIG, BIG)
+        @pl.when(c >= 2)
+        def _():
+            pltpu.make_async_copy(ds_out.at[slot], ds_ref.at[c], ds_sem.at[slot]).wait()
+
+        def leave_ds(k, _):
+            span = pl.ds(pl.multiple_of(k * BIG, BIG), BIG)
+            pltpu.make_async_copy(ds_out.at[slot, span], ds_ref.at[c, span], ds_sem.at[slot]).start()
+            return 0
+
+        def back(u, size):
+            o = pl.multiple_of(u * SMALL, SMALL)
             span = pl.ds(o, size)
-            w = exps[span, :] * (jnp.exp2(tops[pl.ds(t * 8, 8), :][:1] - m) * share)
+            w = exps[span, :] * (jnp.exp2(tops[pl.ds(pl.multiple_of(u * 8, 8), 8), :][:1] - m) * share)
             ds = (w * ((gws[span, :] - delta) * SCALE)).astype(bf16)
-            ds_out[slot, :size] = ds
-            if size < BIG:
-                ds_out[slot, size:] = jnp.zeros((BIG - size, ROWS), bf16)
-            leave_ds(slot, t).start()
+            ds_out[slot, span, :] = ds
             nt = (((1,), (1,)), ((), ()))
-            acc[:LAT, span] += (lax.dot_general(qs_t[:LAT], ds, nt, preferred_element_type=f32)
-                                + lax.dot_general(dos_t[...], w.astype(bf16), nt, preferred_element_type=f32))
-            acc[LAT:, span] += lax.dot_general(qs_t[LAT:KVW], ds, nt, preferred_element_type=f32)
-
-        def bulk_back(t, _):
-            back(t, BIG)
+            acc[:, span] += lax.dot_general(qs_t[:KVW], ds, nt, preferred_element_type=f32)
+            acc[:LAT, span] += lax.dot_general(dos_t[...], w.astype(bf16), nt, preferred_element_type=f32)
+            for k in range(max(size // BIG, 1)):
+                leave_ds(u // 2 + k, 0)
             return 0
 
-        lax.fori_loop(0, bulk, bulk_back, 0)
-        pl.when(odd)(lambda: back(bulk, BIG))
-        pl.when(jnp.logical_not(odd))(lambda: back(bulk, SMALL))
-
-        def blank(t, _):
-            pltpu.make_async_copy(zeros, ds_ref.at[c, pl.ds(t * BIG, BIG)], zero_sem).start()
+        def blank(u, _):
+            ds_out[slot, pl.ds(pl.multiple_of(u * SMALL, SMALL), SMALL), :] = jnp.zeros((SMALL, ROWS), bf16)
             return 0
 
-        lax.fori_loop(bulk + 1, QUARTERS, blank, 0)
-        return made + bulk + 1
-
-    made = lax.fori_loop(0, CHUNKS, chunk, 0)
+        lax.fori_loop(full + 1, TOKENS // SMALL, blank, 0)
+        lax.fori_loop(last // 2 + 1, QUARTERS, leave_ds, 0)
+        lax.fori_loop(0, huge, lambda t, _: back(t * 4, HUGE), 0)
+        lax.fori_loop(0, big, lambda t, _: back(huge * 4, BIG), 0)
+
+        @pl.when(odd)
+        def _():
+            back(last, BIG)
+
+        @pl.when(jnp.logical_not(odd))
+        def _():
+            back(last, SMALL)
+
+        return 0
+
+    lax.fori_loop(0, CHUNKS, chunk, 0)
+    copy_keys.wait()
 
     def leave(j, _):
         o = pl.multiple_of(j * 256, 256)
         keys[pl.ds(o, 256), :KVW] = acc[:, pl.ds(o, 256)].astype(bf16).T
         for i in range(4):
-            pltpu.make_async_copy(keys.at[pl.ds(o + i * RUN, RUN)], part_ref.at[chip_of[j * 4 + i]], out_sem).start()
+            pltpu.make_async_copy(keys.at[pl.ds(o + i * RUN, RUN)], part_ref.at[chip_of[j * 4 + i]], out_sem.at[0]).start()
         return 0
 
     lax.fori_loop(0, TOKENS // 256, leave, 0)
-    copy_kt.wait()
     for slot in range(2):
-        pltpu.make_async_copy(ds_out.at[slot], ds_ref.at[0, pl.ds(0, BIG)], ds_sem.at[slot]).wait()
-
-    def blanked(i, _):
-        pltpu.make_async_copy(zeros, ds_ref.at[0, pl.ds(0, BIG)], zero_sem).wait()
-        return 0
-
-    lax.fori_loop(made, SLICES, blanked, 0)
-    pltpu.make_async_copy(keys, keys, out_sem).wait()
-
-
-def attend(positions, query, out_grad, gathered):
+        pltpu.make_async_copy(ds_out.at[slot], ds_ref.at[0], ds_sem.at[slot]).wait()
+    pltpu.make_async_copy(keys, keys, out_sem.at[0]).wait()
+
+
+def attend(positions, runs, query, out_grad, gathered):
     V, f32, bf16 = pltpu.VMEM, jnp.float32, jnp.bfloat16
     return pl.pallas_call(
         attend_kernel,
-        out_shape=(jax.ShapeDtypeStruct((CHUNKS, TOKENS, ROWS), bf16), jax.ShapeDtypeStruct((KVW, TOKENS), bf16),
+        out_shape=(jax.ShapeDtypeStruct((CHUNKS, TOKENS, ROWS), bf16), jax.ShapeDtypeStruct((TOKENS, PAD), bf16),
                    jax.ShapeDtypeStruct((RUNS, RUN, PAD), bf16)),
-        in_specs=[pl.BlockSpec(memory_space=pltpu.SMEM)] + [pl.BlockSpec(memory_space=pltpu.HBM)] * 3,
+        in_specs=[pl.BlockSpec(memory_space=pltpu.SMEM)] * 2 + [pl.BlockSpec(memory_space=pltpu.HBM)] * 3,
         out_specs=(pl.BlockSpec(memory_space=pltpu.HBM),) * 3,
         scratch_shapes=[
-            pltpu.SMEM((RUNS, 128), jnp.int32), pltpu.SMEM((RUNS,), jnp.int32),
-            V((TOKENS, PAD), bf16), V((KVW, TOKENS), bf16), V((KVW, TOKENS), f32),
-            V((TOKENS, ROWS), f32), V((TOKENS, ROWS), f32), V((QUARTERS * 8, ROWS), f32),
+            pltpu.SMEM((RUNS,), jnp.int32),
+            V((TOKENS, PAD), bf16), V((KVW, TOKENS), f32),
+            V((TOKENS, ROWS), f32), V((TOKENS, ROWS), f32), V((TOKENS // SMALL * 8, ROWS), f32),
             V((ROWS, PAD), bf16), V((PAD, ROWS), bf16), V((ROWS, LAT), bf16), V((LAT, ROWS), bf16),
-            V((2 * RUN, HEADS * KVW), bf16), V((2 * RUN, HEADS * LAT), bf16), V((2, BIG, ROWS), bf16), V((BIG, ROWS), bf16),
-            V((RUNS, 16, 128), bf16), V((RUNS, 128), jnp.int32),
-            pltpu.SemaphoreType.DMA, pltpu.SemaphoreType.DMA((3,)), pltpu.SemaphoreType.DMA, pltpu.SemaphoreType.DMA((2,)),
-            pltpu.SemaphoreType.DMA,
+            V((2 * RUN, HEADS * KVW), bf16), V((2 * RUN, HEADS * LAT), bf16), V((2, TOKENS, ROWS), bf16),
+            pltpu.SemaphoreType.DMA((TOKENS // BIG,)), pltpu.SemaphoreType.DMA((2, CHUNKS)), pltpu.SemaphoreType.DMA((2,)), pltpu.SemaphoreType.DMA((2,)),
         ],
-        compiler_params=pltpu.CompilerParams(vmem_limit_bytes=60 * 2**20),
+        compiler_params=pltpu.CompilerParams(vmem_limit_bytes=62 * 2**20),
         cost_estimate=pl.CostEstimate(flops=46 * 10**9, bytes_accessed=2 * 10**7, transcendentals=10**7),
         name="attend",
-    )(positions, query, out_grad, gathered)
+    )(positions, runs, query, out_grad, gathered)
+
+
+def settle_kernel(qg_in, lg_in, qg_ref, lg_ref, sem):
+    copies = [pltpu.make_async_copy(qg_in.at[pl.ds(i * 32, 32)], qg_ref.at[pl.ds(i * 32, 32)], sem.at[i]) for i in range(4)]
+    copies.append(pltpu.make_async_copy(lg_in, lg_ref, sem.at[4]))
+    for c in copies:
+        c.start()
+    for c in copies:
+        c.wait()
+
+
+def settle(query_grad, latent_grad):
+    return pl.pallas_call(
+        settle_kernel,
+        out_shape=(jax.ShapeDtypeStruct(query_grad.shape, query_grad.dtype), jax.ShapeDtypeStruct(latent_grad.shape, latent_grad.dtype)),
+        in_specs=[pl.BlockSpec(memory_space=pltpu.HBM), pl.BlockSpec(memory_space=pl.ANY)],
+        out_specs=(pl.BlockSpec(memory_space=pltpu.HBM),) * 2,
+        scratch_shapes=[pltpu.SemaphoreType.DMA((5,))],
+        cost_estimate=pl.CostEstimate(flops=0, bytes_accessed=5 * 10**6, transcendentals=0),
+        name="settle",
+    )(query_grad, latent_grad)
 
 
 def per_device(query, latent, out_grad, positions):
-    gathered = gather(positions, latent)
-    ds, keys_t, part = attend(positions, query, out_grad, gathered.reshape(2, RUNS, 32, PAD))
-    latent_grad, query_grad = scatter(part.reshape(4, 4, 4, RUN, PAD), ds, keys_t)
-    return query_grad, latent_grad
+    gathered, runs = gather(positions, latent)
+    ds, keys, part = attend(positions, runs, query, out_grad, gathered.reshape(RUNS, RUN, PAD))
+    latent_grad, query_grad = scatter(part.reshape(4, 4, 4, RUN, PAD), ds, keys)
+    return settle(query_grad, latent_grad)
 
 
 def solution(mesh):

time: 130 us -> 197 us (1.52)
  Pallas kernels: 125 us -> 196 us
  local copies, waits for them, and re-layouts: 3.89 us -> 0 us
    pallas_call x1 -> x2, Pallas kernels: 29.4 us -> 106 us  [the longest x1 75.1 us: settle(): pl.pallas_call(settle_kernel, out_shape=(jax.ShapeDtypeStruct(query_grad....]
    pallas_call x1, Pallas kernels: 42.3 us -> 33.6 us  [attend(): pl.pallas_call(attend_kernel, out_shape=(jax.ShapeDtypeStruct((CHUNKS, TO...]
    unnamed x4 -> x0, local copies, waits for them, and re-layouts: 3.89 us -> none
    pallas_call x1, Pallas kernels: 53.3 us -> 56.6 us  [scatter(): pl.pallas_call(scatter_kernel, out_shape=(jax.ShapeDtypeStruct((32, KVW),...]
where the time goes in v3:
time: 197 us
  Pallas kernels  196 us (99%)
    pallas_call x1, Pallas kernels, settle(): pl.pallas_call(settle_kernel, out_shape=(jax.ShapeDtypeStruct(query_grad....  75.1 us
    pallas_call x1, Pallas kernels, scatter(): pl.pallas_call(scatter_kernel, out_shape=(jax.ShapeDtypeStruct((32, KVW),...  56.6 us
    pallas_call x1, Pallas kernels, attend(): pl.pallas_call(attend_kernel, out_shape=(jax.ShapeDtypeStruct((CHUNKS, TO...  33.6 us
    pallas_call x1, Pallas kernels, gather(): pl.pallas_call(gather_kernel, out_shape=(jax.ShapeDtypeStruct((4, 4, 4, 2...  30.7 us

profile of v3, /device:TPU:0, one launch (start us, length us, event | category | flops | bytes accessed | tf_op | source)
XLA Modules:
  0.0 196.9 jit_solution(3266256006591353228)
XLA Ops:
  0.6 30.7 %gather_latent.1 = (bf16[4,4,4,2,32,640]{5,4,3,2,1,0:T(8,128)(2,1)}, s32[8,128]{1,0:T(8,128)}) custom-call(s32[128]{0:T(128)} %pos_ref.3, bf16[32,576]{1,0:T(8,128)(2,1)} %lat_ref.1), custom_call_target="tpu_custom_call" | custom-call | bytes 10485760 | tf_op jit(solution)/shard_map/gather_latent/pallas_call | solution.py:157
  31.4 33.6 %attend.1 = (bf16[4,4096,512]{2,1,0:T(8,128)(2,1)}, bf16[4096,640]{1,0:T(8,128)(2,1)}, bf16[64,64,640]{2,1,0:T(8,128)(2,1)}) custom-call(s32[128]{0:T(128)} %pos_ref.3, s32[8,128]{1,0:T(8,128)} %get-tuple-element.9.runs_ref, bf16[128,9216]{1,0:T(8,128)(2,1)} %q_ref.1, bf16[128,8192]{1,0:T(8,128)(2,1)} %do_ref.1, bf16[64,64,640]{2,1,0:T(8,128)(2,1)} %bitcast.2), custom_call_target="tpu_custom_call" | custom-call | flops 46000001024 | bytes 20000000 | tf_op jit(solution)/shard_map/attend/pallas_call | solution.py:517
  65.0 56.6 %scatter_latent_grad.1 = (f32[32,576]{1,0:T(8,128)}, bf16[128,9216]{1,0:T(8,128)(2,1)}) custom-call(bf16[4,4,4,64,640]{4,3,2,1,0:T(8,128)(2,1)} %bitcast.3, bf16[4,4096,512]{2,1,0:T(8,128)(2,1)} %get-tuple-element.12.ds_ref, bf16[4096,640]{1,0:T(8,128)(2,1)} %get-tuple-element.13.keys_ref), custom_call_target="tpu_custom_call" | custom-call | flops 10000000000 | bytes 30000000 | tf_op jit(solution)/shard_map/scatter_latent_grad/pallas_call | solution.py:339
  121.6 75.1 %settle.1 = (bf16[128,9216]{1,0:T(8,128)(2,1)}, f32[32,576]{1,0:T(8,128)}) custom-call(bf16[128,9216]{1,0:T(8,128)(2,1)} %get-tuple-element.14.qg_in, f32[32,576]{1,0:T(8,128)} %get-tuple-element.15.lg_in), custom_call_target="tpu_custom_call" | custom-call | bytes 5000000 | tf_op jit(solution)/shard_map/settle/pallas_call | solution.py:547

commit v4 on v3

--- a/solution.py
+++ b/solution.py
@@ -19,10 +19,13 @@
 HUGE, BIG, SMALL = 2048, 1024, 512
 CHUNKS = 2 * HEADS // GROUP
 QUARTERS = TOKENS // BIG
-SLICES = CHUNKS * QUARTERS
-PLAN = (4, 4, 3, 2, 1, 1, 1)
+PIECE = 2048
+PIECES = TOKENS // PIECE
+SLICES = CHUNKS * PIECES
+PLAN = (0, 1, 2, 2, 0, 1)
 MESH = pl.DeviceIdType.MESH
 PARTS = (((0, 1, 2), 0, 256), ((1, 2, 0), 256, 256), ((2, 0, 1), 512, 128))
+SUM_PARTS = (((0, 2, 1), 0, 256), ((1, 2, 0), 256, 256), ((2, 1, 0), 512, 128))
 
 
 def coords():
@@ -193,7 +196,7 @@
     load_keys.start()
 
     def load_ds(i):
-        return pltpu.make_async_copy(ds_ref.at[i // QUARTERS, pl.ds(lax.rem(i, QUARTERS) * BIG, BIG)], ds_in.at[lax.rem(i, 2)], ds_sem.at[lax.rem(i, 2)])
+        return pltpu.make_async_copy(ds_ref.at[i // PIECES, pl.ds(lax.rem(i, PIECES) * PIECE, PIECE)], ds_in.at[lax.rem(i, 2)], ds_sem.at[lax.rem(i, 2)])
 
     load_ds(0).start()
 
@@ -202,14 +205,14 @@
         def _():
             load_ds(i + 1).start()
         load_ds(i).wait()
-        c, k = i // QUARTERS, lax.rem(i, QUARTERS)
+        c, k = i // PIECES, lax.rem(i, PIECES)
 
         @pl.when(k == 0)
         def _():
             qg_t[...] = jnp.zeros_like(qg_t)
-        qg_t[...] += jnp.dot(keys_t[:, pl.ds(pl.multiple_of(k * BIG, BIG), BIG)], ds_in[lax.rem(i, 2)], preferred_element_type=jnp.float32)
-
-        @pl.when(k == QUARTERS - 1)
+        qg_t[...] += jnp.dot(keys_t[:, pl.ds(pl.multiple_of(k * PIECE, PIECE), PIECE)], ds_in[lax.rem(i, 2)], preferred_element_type=jnp.float32)
+
+        @pl.when(k == PIECES - 1)
         def _():
             row = pl.multiple_of((c // 2) * RUN, RUN)
             for h in range(0, GROUP, 2):
@@ -225,7 +228,7 @@
         done_work[0] += n
         lax.fori_loop(first, first + n, slice_of_work, 0)
 
-    greet(place, core)
+    greet(place, core, True)
     count = [0]
     sent = []
 
@@ -239,7 +242,7 @@
 
     sibling = device(place, 1 - core)
     swaps, loads = [], []
-    for n, (order, lane, width) in enumerate(PARTS):
+    for n, (order, lane, width) in enumerate(SUM_PARTS):
         other = part_ref.at[:, :, :, pl.ds(32 * (1 - core), 32), pl.ds(lane, width)]
         swaps.append(copy(other, theirs[n], sibling))
         load = pltpu.make_async_copy(part_ref.at[:, :, :, pl.ds(32 * core, 32), pl.ds(lane, width)], mine[n], sem.at[n])
@@ -256,77 +259,94 @@
     lax.fori_loop(0, TOKENS // 256, turn, 0)
     work(PLAN[0])
     halves = ((0, 16), (16, 16))
-    for phase in range(3):
-        started = []
-        for n, (order, lane, width) in enumerate(PARTS):
-            axis, done = order[phase], order[:phase]
-            dim = dropped(axis, done)
-            k, w, rl, ld = keep[n][phase], wire[n][phase], relay[n][phase], landed[n][phase]
-            me = place[axis]
-            right, left, opp = (lax.rem(me + i, 4) for i in (1, 3, 2))
-            rdev, ldev = device(moved(place, axis, 1), core), device(moved(place, axis, 3), core)
-            if phase == 0:
-                loads[n].wait()
-                swaps[n].wait_recv()
-                def fill(v):
-                    at(k, dim, v)[...] = at(mine[n], dim, v)[...].astype(jnp.float32) + at(theirs[n], dim, v)[...].astype(jnp.float32)
+
+    def parts(phase):
+        for n, (order, lane, width) in enumerate(SUM_PARTS):
+            axis = order[phase]
+            yield n, axis, dropped(axis, order[:phase]), place[axis], lane, width
+
+    started = []
+    for n, axis, dim, me, lane, width in parts(0):
+        k, w, rl, ld = keep[n][0], wire[n][0], relay[n], landed[n][0]
+        right, left, opp = (lax.rem(me + i, 4) for i in (1, 3, 2))
+        rdev, ldev = device(moved(place, axis, 1), core), device(moved(place, axis, 3), core)
+        loads[n].wait()
+        swaps[n].wait_recv()
+
+        def fill(v):
+            at(k, dim, v)[...] = at(mine[n], dim, v)[...].astype(jnp.float32) + at(theirs[n], dim, v)[...].astype(jnp.float32)
+
+        fill(opp)
+        at(w, dim, opp)[...] = at(k, dim, opp)[...].astype(w.dtype)
+        c0 = copy(at(w, dim, opp, halves[0]), rl.at[0], rdev)
+        c1 = copy(at(w, dim, opp, halves[1]), rl.at[1], ldev)
+        fill(right)
+        at(w, dim, right, halves[1])[...] = at(k, dim, right, halves[1])[...].astype(w.dtype)
+        c2 = copy(at(w, dim, right, halves[1]), ld.at[0, 1], rdev)
+        fill(left)
+        at(w, dim, left, halves[0])[...] = at(k, dim, left, halves[0])[...].astype(w.dtype)
+        c3 = copy(at(w, dim, left, halves[0]), ld.at[1, 0], ldev)
+        fill(me)
+        started.append((c0, c1, c2, c3))
+        work(PLAN[1])
+    ended = []
+    for n, axis, dim, me, lane, width in parts(0):
+        k, w, rl, ld = keep[n][0], wire[n][0], relay[n], landed[n][0]
+        right, left = lax.rem(me + 1, 4), lax.rem(me + 3, 4)
+        rdev, ldev = device(moved(place, axis, 1), core), device(moved(place, axis, 3), core)
+        c0, c1, c2, c3 = started[n]
+        c0.wait_recv()
+        at(w, dim, right, halves[0])[...] = (at(k, dim, right, halves[0])[...] + rl[0].astype(jnp.float32)).astype(w.dtype)
+        c4 = copy(at(w, dim, right, halves[0]), ld.at[0, 0], rdev)
+        c1.wait_recv()
+        at(w, dim, left, halves[1])[...] = (at(k, dim, left, halves[1])[...] + rl[1].astype(jnp.float32)).astype(w.dtype)
+        c5 = copy(at(w, dim, left, halves[1]), ld.at[1, 1], ldev)
+        ended.append((c2, c3, c4, c5))
+    work(PLAN[2])
+    going = []
+    for phase in (1, 2):
+        for n, axis, dim, me, lane, width in parts(phase):
+            if phase == 1:
+                for c in ended[n]:
+                    c.wait_recv()
+                ld = landed[n][0]
+                was = list(parts(0))[n]
+                for h in (0, 1):
+                    keep[n][1].at[:, :, pl.ds(*halves[h])][...] = (at(keep[n][0], was[2], was[3], halves[h])[...] + ld[0, h].astype(jnp.float32)) + ld[1, h].astype(jnp.float32)
             else:
-                def fill(v):
-                    pass
-            fill(opp)
-            at(w, dim, opp)[...] = at(k, dim, opp)[...].astype(w.dtype)
-            c0 = copy(at(w, dim, opp, halves[0]), rl.at[0], rdev)
-            c1 = copy(at(w, dim, opp, halves[1]), rl.at[1], ldev)
-            fill(right)
-            at(w, dim, right, halves[1])[...] = at(k, dim, right, halves[1])[...].astype(w.dtype)
-            c2 = copy(at(w, dim, right, halves[1]), ld.at[0, 1], rdev)
-            fill(left)
-            at(w, dim, left, halves[0])[...] = at(k, dim, left, halves[0])[...].astype(w.dtype)
-            c3 = copy(at(w, dim, left, halves[0]), ld.at[1, 0], ldev)
-            fill(me)
-            started.append((c0, c1, c2, c3))
+                for c in going[n]:
+                    c.wait_recv()
+                ld = landed[n][1]
+                was = list(parts(1))[n]
+                keep[n][2][...] = (at(keep[n][1], was[2], was[3])[...] + ld[0].astype(jnp.float32)) + (ld[1].astype(jnp.float32) + ld[2].astype(jnp.float32))
+            k, w, ld = keep[n][phase], wire[n][phase], landed[n][phase]
+            sends = []
+            for slot, by in enumerate((2, 1, 3)):
+                v = lax.rem(me + by, 4)
+                at(w, dim, v)[...] = at(k, dim, v)[...].astype(w.dtype)
+                sends.append(copy(at(w, dim, v), ld.at[slot], device(moved(place, axis, by), core)))
+            if phase == 1:
+                going.append(sends)
+            else:
+                going[n] = sends
         work(PLAN[1 + 2 * phase])
-        ended = []
-        for n, (order, lane, width) in enumerate(PARTS):
-            axis, done = order[phase], order[:phase]
-            dim = dropped(axis, done)
-            k, w, rl, ld = keep[n][phase], wire[n][phase], relay[n][phase], landed[n][phase]
-            me = place[axis]
-            right, left = lax.rem(me + 1, 4), lax.rem(me + 3, 4)
-            rdev, ldev = device(moved(place, axis, 1), core), device(moved(place, axis, 3), core)
-            c0, c1, c2, c3 = started[n]
-            c0.wait_recv()
-            at(w, dim, right, halves[0])[...] = (at(k, dim, right, halves[0])[...] + rl[0].astype(jnp.float32)).astype(w.dtype)
-            c4 = copy(at(w, dim, right, halves[0]), ld.at[0, 0], rdev)
-            c1.wait_recv()
-            at(w, dim, left, halves[1])[...] = (at(k, dim, left, halves[1])[...] + rl[1].astype(jnp.float32)).astype(w.dtype)
-            c5 = copy(at(w, dim, left, halves[1]), ld.at[1, 1], ldev)
-            ended.append((c2, c3, c4, c5))
-        work(PLAN[2 + 2 * phase])
         if phase == 2:
             put = pltpu.make_async_copy(qg_out, qg_ref, qg_sem)
             put.start()
-        for n, (order, lane, width) in enumerate(PARTS):
-            axis, done = order[phase], order[:phase]
-            dim = dropped(axis, done)
-            k, ld = keep[n][phase], landed[n][phase]
-            for c in ended[n]:
-                c.wait_recv()
-            for h in (0, 1):
-                total = (at(k, dim, place[axis], halves[h])[...] + ld[0, h].astype(jnp.float32)) + ld[1, h].astype(jnp.float32)
-                if phase < 2:
-                    to = keep[n][phase + 1]
-                    to.at[tuple([slice(None)] * (2 - phase) + [pl.ds(*halves[h])])][...] = total
-                else:
-                    real = min(width, KVW - lane)
-                    out_ref[pl.ds(*halves[h]), pl.ds(lane, real)] = total[:, :real]
+    for n, axis, dim, me, lane, width in parts(2):
+        for c in going[n]:
+            c.wait_recv()
+        ld = landed[n][2]
+        total = (at(keep[n][2], 0, me)[...] + ld[0]) + (ld[1] + ld[2])
+        real = min(width, KVW - lane)
+        out_ref[:, pl.ds(lane, real)] = total[:, :real]
     put.wait()
     for s in sent:
         s.wait_send()
 
 
-N_SCATTER = 3 + 9 * 6
-WIRES = (jnp.bfloat16, jnp.float32, jnp.float32)
+N_SCATTER = 3 + 3 * (6 + 3 + 3)
+WIRES = (jnp.bfloat16, jnp.bfloat16, jnp.float32)
 
 
 def scatter(part, ds, keys):
@@ -334,8 +354,8 @@
     mine = [V((4, 4, 4, 32, w), bf16) for _, _, w in PARTS]
     keep = [[V((4,) * (3 - p) + (32, w), f32) for p in range(3)] for _, _, w in PARTS]
     wire = [[V((4,) * (3 - p) + (32, w), WIRES[p]) for p in range(3)] for _, _, w in PARTS]
-    relay = [[V((2,) + (4,) * (2 - p) + (16, w), WIRES[p]) for p in range(3)] for _, _, w in PARTS]
-    landed = [[V((2, 2) + (4,) * (2 - p) + (16, w), WIRES[p]) for p in range(3)] for _, _, w in PARTS]
+    relay = [V((2, 4, 4, 16, w), WIRES[0]) for _, _, w in PARTS]
+    landed = [[V((2, 2, 4, 4, 16, w), WIRES[0]), V((3, 4, 32, w), WIRES[1]), V((3, 32, w), WIRES[2])] for _, _, w in PARTS]
     return pl.pallas_call(
         scatter_kernel,
         out_shape=(jax.ShapeDtypeStruct((32, KVW), f32), jax.ShapeDtypeStruct((2 * RUN, HEADS * KVW), bf16)),
@@ -343,7 +363,7 @@
         out_specs=(pl.BlockSpec(memory_space=pltpu.VMEM), pl.BlockSpec(memory_space=pltpu.HBM)),
         scratch_shapes=[
             mine, list(mine), keep, wire, relay, landed,
-            V((TOKENS, PAD), bf16), V((KVW, TOKENS), bf16), V((2, BIG, ROWS), bf16), V((KVW, ROWS), f32), V((2 * RUN, HEADS * KVW), bf16),
+            V((TOKENS, PAD), bf16), V((KVW, TOKENS), bf16), V((2, PIECE, ROWS), bf16), V((KVW, ROWS), f32), V((2 * RUN, HEADS * KVW), bf16),
             pltpu.SemaphoreType.DMA((3,)), pltpu.SemaphoreType.DMA, pltpu.SemaphoreType.DMA((2,)), pltpu.SemaphoreType.DMA,
             pltpu.SemaphoreType.DMA((N_SCATTER,)),
             pltpu.SemaphoreType.DMA((N_SCATTER,)),
@@ -534,13 +554,18 @@
     )(positions, runs, query, out_grad, gathered)
 
 
-def settle_kernel(qg_in, lg_in, qg_ref, lg_ref, sem):
-    copies = [pltpu.make_async_copy(qg_in.at[pl.ds(i * 32, 32)], qg_ref.at[pl.ds(i * 32, 32)], sem.at[i]) for i in range(4)]
-    copies.append(pltpu.make_async_copy(lg_in, lg_ref, sem.at[4]))
-    for c in copies:
-        c.start()
-    for c in copies:
-        c.wait()
+def settle_kernel(qg_in, lg_in, qg_ref, lg_ref, qg_buf, lg_buf, sem):
+    pieces = [(qg_in.at[pl.ds(i * 32, 32)], qg_buf.at[pl.ds(i * 32, 32)], qg_ref.at[pl.ds(i * 32, 32)]) for i in range(4)]
+    pieces.append((lg_in, lg_buf, lg_ref))
+    loads = [pltpu.make_async_copy(a, b, sem.at[0, i]) for i, (a, b, _) in enumerate(pieces)]
+    stores = [pltpu.make_async_copy(b, c, sem.at[1, i]) for i, (_, b, c) in enumerate(pieces)]
+    for load in loads:
+        load.start()
+    for load, store in zip(loads, stores):
+        load.wait()
+        store.start()
+    for store in stores:
+        store.wait()
 
 
 def settle(query_grad, latent_grad):
@@ -549,7 +574,7 @@
         out_shape=(jax.ShapeDtypeStruct(query_grad.shape, query_grad.dtype), jax.ShapeDtypeStruct(latent_grad.shape, latent_grad.dtype)),
         in_specs=[pl.BlockSpec(memory_space=pltpu.HBM), pl.BlockSpec(memory_space=pl.ANY)],
         out_specs=(pl.BlockSpec(memory_space=pltpu.HBM),) * 2,
-        scratch_shapes=[pltpu.SemaphoreType.DMA((5,))],
+        scratch_shapes=[pltpu.VMEM(query_grad.shape, query_grad.dtype), pltpu.VMEM(latent_grad.shape, latent_grad.dtype), pltpu.SemaphoreType.DMA((2, 5))],
         cost_estimate=pl.CostEstimate(flops=0, bytes_accessed=5 * 10**6, transcendentals=0),
         name="settle",
     )(query_grad, latent_grad)

time: 197 us -> 118 us (0.60)
  Pallas kernels: 196 us -> 117 us
    pallas_call x1, Pallas kernels: 75.1 us -> 2.56 us  [settle(): pl.pallas_call(settle_kernel, out_shape=(jax.ShapeDtypeStruct(query_grad....]
    pallas_call x1, Pallas kernels: 33.6 us -> 24.7 us  [attend(): pl.pallas_call(attend_kernel, out_shape=(jax.ShapeDtypeStruct((CHUNKS, TO...]
where the time goes in v4:
time: 118 us; the launch traced here: 117 us
  Pallas kernels  117 us (99%)
    pallas_call x1, Pallas kernels, scatter(): pl.pallas_call(scatter_kernel, out_shape=(jax.ShapeDtypeStruct((32, KVW),...  58.6 us
    pallas_call x1, Pallas kernels, gather(): pl.pallas_call(gather_kernel, out_shape=(jax.ShapeDtypeStruct((4, 4, 4, 2...  30.7 us
    pallas_call x1, Pallas kernels, attend(): pl.pallas_call(attend_kernel, out_shape=(jax.ShapeDtypeStruct((CHUNKS, TO...  24.7 us
    pallas_call x1, Pallas kernels, settle(): pl.pallas_call(settle_kernel, out_shape=(jax.ShapeDtypeStruct(query_grad....  2.56 us

profile of v4, /device:TPU:0, one launch (start us, length us, event | category | flops | bytes accessed | tf_op | source)
XLA Modules:
  0.0 117.4 jit_solution(4890432262007854962)
XLA Ops:
  0.6 30.7 %gather_latent.1 = (bf16[4,4,4,2,32,640]{5,4,3,2,1,0:T(8,128)(2,1)}, s32[8,128]{1,0:T(8,128)}) custom-call(s32[128]{0:T(128)} %pos_ref.3, bf16[32,576]{1,0:T(8,128)(2,1)} %lat_ref.1), custom_call_target="tpu_custom_call" | custom-call | bytes 10485760 | tf_op jit(solution)/shard_map/gather_latent/pallas_call | solution.py:160
  31.4 24.7 %attend.1 = (bf16[4,4096,512]{2,1,0:T(8,128)(2,1)}, bf16[4096,640]{1,0:T(8,128)(2,1)}, bf16[64,64,640]{2,1,0:T(8,128)(2,1)}) custom-call(s32[128]{0:T(128)} %pos_ref.3, s32[8,128]{1,0:T(8,128)} %get-tuple-element.9.runs_ref, bf16[128,9216]{1,0:T(8,128)(2,1)} %q_ref.1, bf16[128,8192]{1,0:T(8,128)(2,1)} %do_ref.1, bf16[64,64,640]{2,1,0:T(8,128)(2,1)} %bitcast.2), custom_call_target="tpu_custom_call" | custom-call | flops 46000001024 | bytes 20000000 | tf_op jit(solution)/shard_map/attend/pallas_call | solution.py:537
  56.1 58.6 %scatter_latent_grad.1 = (f32[32,576]{1,0:T(8,128)}, bf16[128,9216]{1,0:T(8,128)(2,1)}) custom-call(bf16[4,4,4,64,640]{4,3,2,1,0:T(8,128)(2,1)} %bitcast.3, bf16[4,4096,512]{2,1,0:T(8,128)(2,1)} %get-tuple-element.12.ds_ref, bf16[4096,640]{1,0:T(8,128)(2,1)} %get-tuple-element.13.keys_ref), custom_call_target="tpu_custom_call" | custom-call | flops 10000000000 | bytes 30000000 | tf_op jit(solution)/shard_map/scatter_latent_grad/pallas_call | solution.py:359
  114.7 2.6 %settle.1 = (bf16[128,9216]{1,0:T(8,128)(2,1)}, f32[32,576]{1,0:T(8,128)}) custom-call(bf16[128,9216]{1,0:T(8,128)(2,1)} %get-tuple-element.14.qg_in, f32[32,576]{1,0:T(8,128)} %get-tuple-element.15.lg_in), custom_call_target="tpu_custom_call" | custom-call | bytes 5000000 | tf_op jit(solution)/shard_map/settle/pallas_call | solution.py:572

commit v5 on v4

--- a/solution.py
+++ b/solution.py
@@ -16,7 +16,7 @@
 HEADS = 16
 GROUP = 8
 ROWS = GROUP * RUN
-HUGE, BIG, SMALL = 2048, 1024, 512
+HUGE, BIG, SMALL = 2048, 1024, 256
 CHUNKS = 2 * HEADS // GROUP
 QUARTERS = TOKENS // BIG
 PIECE = 2048
@@ -65,12 +65,11 @@
     put = pltpu.make_async_copy(own, out_ref.at[place[0], place[1], place[2], core], sem)
     put.start()
     greet(place, core, True)
-    put.wait()
     sent = []
 
-    def copy(ref, dev):
+    def copy(ref, dev, source=None):
         i = len(sent)
-        c = pltpu.make_async_remote_copy(ref, ref, send.at[i], recv.at[i], device_id=dev, device_id_type=MESH)
+        c = pltpu.make_async_remote_copy(ref if source is None else source, ref, send.at[i], recv.at[i], device_id=dev, device_id_type=MESH)
         c.start()
         sent.append(c)
         return c
@@ -89,7 +88,7 @@
     def spread(p, d1):
         order, lane, width = PARTS[p]
         for by in steps:
-            two[p, d1, by] = copy(shards(order, lane, width, d1, 0, 0), device(moved(place, order[1], by), core))
+            two[p, d1, by] = copy(shards(order, lane, width, d1, 0, 0), device(moved(place, order[1], by), core), None if d1 else own.at[:, pl.ds(lane, width)])
 
     def shift(p, d2):
         order, lane, width = PARTS[p]
@@ -111,13 +110,14 @@
     for p in n:
         order, lane, width = PARTS[p]
         for by in steps:
-            one[p, by] = copy(shards(order, lane, width, 0, 0, 0), device(moved(place, order[0], by), core))
+            one[p, by] = copy(shards(order, lane, width, 0, 0, 0), device(moved(place, order[0], by), core), own.at[:, pl.ds(lane, width)])
     for p in n:
         spread(p, 0)
     for by in steps:
         for p in n:
             one[p, by].wait_recv()
             spread(p, {1: 3, 3: 1, 2: 2}[by])
+    put.wait()
     for p in n:
         shift(p, 0)
     for d2 in (3, 1, 2):
@@ -134,13 +134,14 @@
         order, lane, width = PARTS[p]
         twins.append(copy(shards(order, lane, width, None, None, 3), sibling))
         twins.append(copy(shards(order, lane, width, None, None, 1), sibling))
-    for p in (2, 0, 1):
+    tagged = [p for p in n if PARTS[p][1] == LAT][0]
+    for p in (tagged, *[p for p in n if p != tagged]):
         order, lane, width = PARTS[p]
         for d2 in (0, 3, 1, 2):
             three[p, d2, 4].wait_recv()
             three[p, d2, 5].wait_recv()
             twins.append(copy(shards(order, lane, width, None, d2, 2), sibling))
-        if p == 2:
+        if p == tagged:
             load_tags = pltpu.make_async_copy(out_ref.at[:, :, :, core, pl.ds(0, 16), pl.ds(LAT, 128)], tags, sem)
             load_tags.start()
     load_tags.wait()
@@ -153,7 +154,7 @@
         s.wait_send()
 
 
-N_GATHER = 3 * (3 + 12 + 8 + 1 + 8 + 2 + 4)
+N_GATHER = len(PARTS) * (3 + 12 + 8 + 1 + 8 + 2 + 4)
 
 
 def gather(positions, latent):
@@ -345,17 +346,17 @@
         s.wait_send()
 
 
-N_SCATTER = 3 + 3 * (6 + 3 + 3)
+N_SCATTER = len(SUM_PARTS) * (1 + 6 + 3 + 3)
 WIRES = (jnp.bfloat16, jnp.bfloat16, jnp.float32)
 
 
 def scatter(part, ds, keys):
     V, f32, bf16 = pltpu.VMEM, jnp.float32, jnp.bfloat16
-    mine = [V((4, 4, 4, 32, w), bf16) for _, _, w in PARTS]
-    keep = [[V((4,) * (3 - p) + (32, w), f32) for p in range(3)] for _, _, w in PARTS]
-    wire = [[V((4,) * (3 - p) + (32, w), WIRES[p]) for p in range(3)] for _, _, w in PARTS]
-    relay = [V((2, 4, 4, 16, w), WIRES[0]) for _, _, w in PARTS]
-    landed = [[V((2, 2, 4, 4, 16, w), WIRES[0]), V((3, 4, 32, w), WIRES[1]), V((3, 32, w), WIRES[2])] for _, _, w in PARTS]
+    mine = [V((4, 4, 4, 32, w), bf16) for _, _, w in SUM_PARTS]
+    keep = [[V((4,) * (3 - p) + (32, w), f32) for p in range(3)] for _, _, w in SUM_PARTS]
+    wire = [[V((4,) * (3 - p) + (32, w), WIRES[p]) for p in range(3)] for _, _, w in SUM_PARTS]
+    relay = [V((2, 4, 4, 16, w), WIRES[0]) for _, _, w in SUM_PARTS]
+    landed = [[V((2, 2, 4, 4, 16, w), WIRES[0]), V((3, 4, 32, w), WIRES[1]), V((3, 32, w), WIRES[2])] for _, _, w in SUM_PARTS]
     return pl.pallas_call(
         scatter_kernel,
         out_shape=(jax.ShapeDtypeStruct((32, KVW), f32), jax.ShapeDtypeStruct((2 * RUN, HEADS * KVW), bf16)),
@@ -364,7 +365,7 @@
         scratch_shapes=[
             mine, list(mine), keep, wire, relay, landed,
             V((TOKENS, PAD), bf16), V((KVW, TOKENS), bf16), V((2, PIECE, ROWS), bf16), V((KVW, ROWS), f32), V((2 * RUN, HEADS * KVW), bf16),
-            pltpu.SemaphoreType.DMA((3,)), pltpu.SemaphoreType.DMA, pltpu.SemaphoreType.DMA((2,)), pltpu.SemaphoreType.DMA,
+            pltpu.SemaphoreType.DMA((len(SUM_PARTS),)), pltpu.SemaphoreType.DMA, pltpu.SemaphoreType.DMA((2,)), pltpu.SemaphoreType.DMA,
             pltpu.SemaphoreType.DMA((N_SCATTER,)),
             pltpu.SemaphoreType.DMA((N_SCATTER,)),
         ],
@@ -433,11 +434,11 @@
         qs_t[...] = qs[...].T
         dos_t[...] = dos[...].T
         full = run // (SMALL // RUN)
-        huge = full // 4
-        rest = lax.rem(full, 4)
-        big = rest // 2
-        odd = lax.rem(rest, 2) == 1
-        last = huge * 4 + big * 2
+        huge = full // (HUGE // SMALL)
+        rest = lax.rem(full, HUGE // SMALL)
+        big = rest // (BIG // SMALL)
+        over = lax.rem(rest, BIG // SMALL)
+        last = full - over
 
         def scan(u, size, masked, carry):
             m, l, d = carry
@@ -445,7 +446,7 @@
             @pl.when(c == 0)
             def _():
                 for i in range(max(size // BIG, 1)):
-                    await_keys(u // 2 + i, 0)
+                    await_keys(u // (BIG // SMALL) + i, 0)
             o = pl.multiple_of(u * SMALL, SMALL)
             tile = keys[pl.ds(o, size), :]
             s = jnp.dot(tile, qs_t[...], preferred_element_type=f32)
@@ -464,13 +465,13 @@
             return top, l * a + jnp.sum(e, axis=0, keepdims=True), d * a + jnp.sum(e * g, axis=0, keepdims=True)
 
         start = (jnp.full((1, ROWS), MASKED, f32), jnp.zeros((1, ROWS), f32), jnp.zeros((1, ROWS), f32))
-        carry = lax.fori_loop(0, huge, lambda t, s: scan(t * 4, HUGE, False, s), start)
-        carry = lax.fori_loop(0, big, lambda t, s: scan(huge * 4, BIG, False, s), carry)
-        m, l, d = lax.cond(odd, lambda: scan(last, BIG, True, carry), lambda: scan(last, SMALL, True, carry))
+        carry = lax.fori_loop(0, huge, lambda t, s: scan(t * (HUGE // SMALL), HUGE, False, s), start)
+        carry = lax.fori_loop(0, big, lambda t, s: scan(huge * (HUGE // SMALL), BIG, False, s), carry)
+        m, l, d = lax.switch(over, [lambda n=n: scan(last, n * SMALL, True, carry) for n in range(1, BIG // SMALL + 1)])
 
         @pl.when(c == 0)
         def _():
-            lax.fori_loop(last // 2 + 1, TOKENS // BIG, await_keys, 0)
+            lax.fori_loop(last // (BIG // SMALL) + 1, TOKENS // BIG, await_keys, 0)
             copy_keys.start()
         share = 1.0 / l
         delta = d * share
@@ -494,7 +495,7 @@
             acc[:, span] += lax.dot_general(qs_t[:KVW], ds, nt, preferred_element_type=f32)
             acc[:LAT, span] += lax.dot_general(dos_t[...], w.astype(bf16), nt, preferred_element_type=f32)
             for k in range(max(size // BIG, 1)):
-                leave_ds(u // 2 + k, 0)
+                leave_ds(u // (BIG // SMALL) + k, 0)
             return 0
 
         def blank(u, _):
@@ -502,17 +503,10 @@
             return 0
 
         lax.fori_loop(full + 1, TOKENS // SMALL, blank, 0)
-        lax.fori_loop(last // 2 + 1, QUARTERS, leave_ds, 0)
-        lax.fori_loop(0, huge, lambda t, _: back(t * 4, HUGE), 0)
-        lax.fori_loop(0, big, lambda t, _: back(huge * 4, BIG), 0)
-
-        @pl.when(odd)
-        def _():
-            back(last, BIG)
-
-        @pl.when(jnp.logical_not(odd))
-        def _():
-            back(last, SMALL)
+        lax.fori_loop(last // (BIG // SMALL) + 1, QUARTERS, leave_ds, 0)
+        lax.fori_loop(0, huge, lambda t, _: back(t * (HUGE // SMALL), HUGE), 0)
+        lax.fori_loop(0, big, lambda t, _: back(huge * (HUGE // SMALL), BIG), 0)
+        lax.switch(over, [lambda n=n: back(last, n * SMALL) for n in range(1, BIG // SMALL + 1)])
 
         return 0
 
@@ -555,7 +549,7 @@
 
 
 def settle_kernel(qg_in, lg_in, qg_ref, lg_ref, qg_buf, lg_buf, sem):
-    pieces = [(qg_in.at[pl.ds(i * 32, 32)], qg_buf.at[pl.ds(i * 32, 32)], qg_ref.at[pl.ds(i * 32, 32)]) for i in range(4)]
+    pieces = [(qg_in.at[pl.ds(i * 16, 16)], qg_buf.at[pl.ds(i * 16, 16)], qg_ref.at[pl.ds(i * 16, 16)]) for i in range(8)]
     pieces.append((lg_in, lg_buf, lg_ref))
     loads = [pltpu.make_async_copy(a, b, sem.at[0, i]) for i, (a, b, _) in enumerate(pieces)]
     stores = [pltpu.make_async_copy(b, c, sem.at[1, i]) for i, (_, b, c) in enumerate(pieces)]
@@ -574,7 +568,7 @@
         out_shape=(jax.ShapeDtypeStruct(query_grad.shape, query_grad.dtype), jax.ShapeDtypeStruct(latent_grad.shape, latent_grad.dtype)),
         in_specs=[pl.BlockSpec(memory_space=pltpu.HBM), pl.BlockSpec(memory_space=pl.ANY)],
         out_specs=(pl.BlockSpec(memory_space=pltpu.HBM),) * 2,
-        scratch_shapes=[pltpu.VMEM(query_grad.shape, query_grad.dtype), pltpu.VMEM(latent_grad.shape, latent_grad.dtype), pltpu.SemaphoreType.DMA((2, 5))],
+        scratch_shapes=[pltpu.VMEM(query_grad.shape, query_grad.dtype), pltpu.VMEM(latent_grad.shape, latent_grad.dtype), pltpu.SemaphoreType.DMA((2, 9))],
         cost_estimate=pl.CostEstimate(flops=0, bytes_accessed=5 * 10**6, transcendentals=0),
         name="settle",
     )(query_grad, latent_grad)

time: 118 us -> 114 us (0.966)
  Pallas kernels: 117 us -> 113 us
    pallas_call x1, Pallas kernels: 58.6 us -> 31.8 us  [scatter(): pl.pallas_call(scatter_kernel, out_shape=(jax.ShapeDtypeStruct((32, KVW),...]
    pallas_call x1, Pallas kernels: 24.7 us -> 48.2 us  [attend(): pl.pallas_call(attend_kernel, out_shape=(jax.ShapeDtypeStruct((CHUNKS, TO...]
where the time goes in v5:
time: 114 us
  Pallas kernels  113 us (99%)
    pallas_call x1, Pallas kernels, attend(): pl.pallas_call(attend_kernel, out_shape=(jax.ShapeDtypeStruct((CHUNKS, TO...  48.2 us
    pallas_call x1, Pallas kernels, scatter(): pl.pallas_call(scatter_kernel, out_shape=(jax.ShapeDtypeStruct((32, KVW),...  31.8 us
    pallas_call x1, Pallas kernels, gather(): pl.pallas_call(gather_kernel, out_shape=(jax.ShapeDtypeStruct((4, 4, 4, 2...  30.5 us
    pallas_call x1, Pallas kernels, settle(): pl.pallas_call(settle_kernel, out_shape=(jax.ShapeDtypeStruct(query_grad....  2.53 us

profile of v5, /device:TPU:0, one launch (start us, length us, event | category | flops | bytes accessed | tf_op | source)
XLA Modules:
  0.0 113.9 jit_solution(954322075000969242)
XLA Ops:
  0.6 30.5 %gather_latent.1 = (bf16[4,4,4,2,32,640]{5,4,3,2,1,0:T(8,128)(2,1)}, s32[8,128]{1,0:T(8,128)}) custom-call(s32[128]{0:T(128)} %pos_ref.3, bf16[32,576]{1,0:T(8,128)(2,1)} %lat_ref.1), custom_call_target="tpu_custom_call" | custom-call | bytes 10485760 | tf_op jit(solution)/shard_map/gather_latent/pallas_call | solution.py:161
  31.1 48.2 %attend.1 = (bf16[4,4096,512]{2,1,0:T(8,128)(2,1)}, bf16[4096,640]{1,0:T(8,128)(2,1)}, bf16[64,64,640]{2,1,0:T(8,128)(2,1)}) custom-call(s32[128]{0:T(128)} %pos_ref.3, s32[8,128]{1,0:T(8,128)} %get-tuple-element.9.runs_ref, bf16[128,9216]{1,0:T(8,128)(2,1)} %q_ref.1, bf16[128,8192]{1,0:T(8,128)(2,1)} %do_ref.1, bf16[64,64,640]{2,1,0:T(8,128)(2,1)} %bitcast.2), custom_call_target="tpu_custom_call" | custom-call | flops 46000001024 | bytes 20000000 | tf_op jit(solution)/shard_map/attend/pallas_call | solution.py:531
  79.4 31.8 %scatter_latent_grad.1 = (f32[32,576]{1,0:T(8,128)}, bf16[128,9216]{1,0:T(8,128)(2,1)}) custom-call(bf16[4,4,4,64,640]{4,3,2,1,0:T(8,128)(2,1)} %bitcast.3, bf16[4,4096,512]{2,1,0:T(8,128)(2,1)} %get-tuple-element.12.ds_ref, bf16[4096,640]{1,0:T(8,128)(2,1)} %get-tuple-element.13.keys_ref), custom_call_target="tpu_custom_call" | custom-call | flops 10000000000 | bytes 30000000 | tf_op jit(solution)/shard_map/scatter_latent_grad/pallas_call | solution.py:360
  111.2 2.5 %settle.1 = (bf16[128,9216]{1,0:T(8,128)(2,1)}, f32[32,576]{1,0:T(8,128)}) custom-call(bf16[128,9216]{1,0:T(8,128)(2,1)} %get-tuple-element.14.qg_in, f32[32,576]{1,0:T(8,128)} %get-tuple-element.15.lg_in), custom_call_target="tpu_custom_call" | custom-call | bytes 5000000 | tf_op jit(solution)/shard_map/settle/pallas_call | solution.py:566
